TPU v7x, 256 devices: a whole 4x4x8 slice. The times are simulated.
256 devices in a mesh: row: 32 (over z_hi, x, core), col: 8 (over z_lo, y).
Axes of the slice: x: 4, y: 4, z: 8 (z_hi: 4, z_lo: 2; z = z_hi * 2 + z_lo), core: 2. Of those that a mesh axis runs over, the one named last changes fastest.
Arguments:
- planes: bfloat16 [4, 448, 896], P(None, 'row', 'col'), may hold values from -6 to 6
- pattern: int32 [1], replicated, may hold values from 0 to 3
- candidate: int32 [5], replicated, may hold values from 0 to 3
- stem_bank: bfloat16 [4, 9, 64, 4], replicated, may hold values from -1 to 1
- layer_bank: bfloat16 [4, 4, 9, 64, 64], replicated, may hold values from -0.25 to 0.25
- embed_weight: bfloat16 [64, 128], replicated, may hold values from -0.75 to 0.75
- norm_gains: float32 [5, 128], replicated, may hold values from 0.1 to 1.9
- qkv_weight: bfloat16 [2, 128, 384], replicated, may hold values from -4 to 4, as said below
- proj_weight: bfloat16 [2, 128, 128], replicated, may hold values from -0.5 to 0.5
- rel_table: float32 [2, 4, 169], replicated, may hold values from -4 to 4
- fc1_weight: bfloat16 [2, 128, 512], replicated, may hold values from -0.5 to 0.5
- fc2_weight: bfloat16 [2, 512, 128], replicated, may hold values from -0.25 to 0.25
- labels: int32 [448, 896], P('row', 'col'), may hold values from 1 to 4
Outputs:
- features: bfloat16 [448, 896, 128], P('row', 'col')
Inputs may be any that keep to these rules, and one draw needn't show every extreme that they name: `pattern`: 0 RGGB, 1 GRBG, 2 GBRG, 3 BGGR. `labels`: sites attend only to sites of the same label. `qkv_weight`: entries of mean 0, of scale about 1 / sqrt(128) on the values.
All inputs are finite; a program needn't handle non-finite values.
Results may differ from a plain program's by a relative error of at most 0.025.
Values may be sent and summed in bfloat16 or wider, within the bound.
No kernel may reach another device: no remote copies, remote signals or barrier semaphores. Data moves between devices by JAX's collectives and lax.ppermute only.
A program may use at most 128 MiB of HBM per device.

v0:
```python
import functools

import jax
import jax.numpy as jnp
from jax import lax
from jax.experimental import pallas as pl
from jax.experimental.pallas import tpu as pltpu
from jax.sharding import PartitionSpec as P

D = 128
HEADS = 4
HD = 32
WIN = 7
LAYERS = 5
C = 64

EPSILON = 1e-05

RIM = 12
F32 = jnp.float32
BF16 = jnp.bfloat16
NEG = -1e30
EXPS = HD ** (-0.5) * 1.4426950408889634


def norm(values, scales):
    centre = jnp.mean(values, -1, keepdims=True)
    centred = values - centre
    spread = jnp.mean(centred * centred, -1, keepdims=True)
    return centred * lax.rsqrt(spread + EPSILON) * scales


def dot(a, b):
    return jnp.dot(a, b, preferred_element_type=F32)


def silu(v):
    half = 0.5 * v
    return half + half * jnp.tanh(half)


def gelu(v):
    return 0.5 * v * (1.0 + lax.erf(v * 0.7071067811865476))


def kernel(
    trows,
    tcols,
    nrows,
    ncols,
    place_ref,
    planes_ref,
    wst_ref,
    wl_ref,
    e2_ref,
    gains_ref,
    qkv_ref,
    proj_ref,
    bias_ref,
    fc1_ref,
    fc2_ref,
    out_ref,
    raw,
    state,
    act_a,
    act_b,
    colmask,
    labels,
    t0,
    h1,
    h2,
):
    frows = trows + 2 * RIM
    fcols = tcols + 2 * RIM + 8
    pairs = frows // 2
    brows = trows + 2 * WIN
    wins0 = tcols // WIN + 2
    wins1 = tcols // WIN + 1

    row_at = place_ref[0] * trows - RIM
    col_at = place_ref[1] * tcols - RIM
    lane = lax.broadcasted_iota(jnp.int32, (1, 128), 1)
    low = lane < C

    raw[...] = jnp.zeros_like(raw)
    for c in range(4):
        raw[c, 8 : 8 + frows, :] = planes_ref[c].astype(F32)
    act_a[0] = jnp.zeros_like(act_a[0])
    act_b[0] = jnp.zeros_like(act_b[0])
    act_a[pairs + 1] = jnp.zeros_like(act_a[0])
    act_b[pairs + 1] = jnp.zeros_like(act_b[0])
    gcol = lax.broadcasted_iota(jnp.int32, (fcols, 128), 0) + col_at
    colmask[...] = ((gcol >= 0) & (gcol < ncols * tcols)).astype(F32)

    lab = planes_ref[4].astype(F32) + 1.0
    lab = jnp.concatenate([lab, jnp.zeros((2, fcols), F32)], 0).T
    for r in range(brows):
        labels[r, 0:fcols, :] = jnp.broadcast_to(lab[:, 5 + r : 6 + r], (fcols, 128))

    def rowmask(k):
        g = row_at + 2 * k
        ok0 = jnp.logical_and(g >= 0, g < nrows * trows).astype(F32)
        ok1 = jnp.logical_and(g >= -1, g < nrows * trows - 1).astype(F32)
        return jnp.where(low, ok0, ok1)

    def gathered(y):
        return (
            pltpu.roll(y[:, 0:128], 1, 0)
            + y[:, 128:256]
            + pltpu.roll(y[:, 256:384], fcols - 1, 0)
        )

    def act_of(x, k):
        return (silu(x) * (colmask[...] * rowmask(k))).astype(BF16)

    def stem(g, _):
        rows = [raw[c, pl.ds(pl.multiple_of(8 * g, 8), 24), :] for c in range(4)]
        for i in range(4):
            k = 4 * g + i
            lhs = jnp.concatenate([v[2 * i + 7 : 2 * i + 15] for v in rows], 0).astype(BF16)
            y = lax.dot_general(
                lhs, wst_ref[...], (((0,), (0,)), ((), ())), preferred_element_type=F32
            )
            x = gathered(y)
            state[k] = x
            act_a[k + 1] = act_of(x, k)
        return 0

    lax.fori_loop(0, (pairs + 3) // 4, stem, 0)

    spans = [(1, pairs, 6), (1, pairs, 6), (2, pairs - 2, 5), (2, pairs - 2, 5)]
    bufs = [act_a, act_b]
    for layer in range(LAYERS - 1):
        src, dst = bufs[layer % 2], bufs[(layer + 1) % 2]
        lo, hi, many = spans[layer]

        def conv(i, _, layer=layer, src=src, dst=dst, lo=lo, many=many):
            k0 = lo + many * i
            lhs = jnp.concatenate(
                [
                    jnp.concatenate(
                        [src[k0 + j + 1], jnp.where(low, src[k0 + j + 2], src[k0 + j])], 1
                    )
                    for j in range(many)
                ],
                0,
            )
            y = dot(lhs, wl_ref[layer])
            xs = []
            for j in range(many):
                k = k0 + j
                x = state[k] + gathered(y[fcols * j : fcols * j + fcols])
                if layer < LAYERS - 2:
                    state[k] = x
                    dst[k + 1] = act_of(x, k)
                else:
                    xs.append(x)
            if layer == LAYERS - 2:
                z = dot(jnp.concatenate(xs, 0).astype(BF16), e2_ref[...])
                g = gains_ref[0:1, :]
                for j in range(many):
                    r = 2 * (k0 + j) - 4
                    zz = z[fcols * j : fcols * j + fcols]
                    t0[r, 0:fcols, :] = norm(zz[:, 0:128], g).astype(BF16).astype(F32)
                    t0[r + 1, 0:fcols, :] = norm(zz[:, 128:256], g).astype(BF16).astype(F32)
            return 0

        lax.fori_loop(0, (hi - lo) // many, conv, 0)

    token = lax.broadcasted_iota(jnp.int32, (56, 128), 0)
    pad = (token & 7) == 7
    diag = (lax.broadcasted_iota(jnp.int32, (56, 128), 1) & 63) == token
    hm = [((lane >= 32 * h) & (lane < 32 * h + 32)) for h in range(HEADS)]
    hst = jnp.concatenate(
        [jnp.broadcast_to(m.astype(F32), (64, 128)) for m in hm], 0
    ).astype(BF16)
    even = (lane & 32) == 0
    zero8 = jnp.zeros((8, 128), F32)

    def attend(block, src, src_row, src_cols, lab_row, dst, dst_row, dst_cols):
        count = len(src_cols)
        x = jnp.concatenate(
            [src[pl.ds(src_row, 7), c : c + 8, :].reshape(56, 128) for c in src_cols], 0
        )
        y = norm(x, gains_ref[1 + 2 * block : 2 + 2 * block, :]).astype(BF16)
        qkv = dot(y, qkv_ref[block])
        scores, values = [], []
        for w in range(count):
            rows = slice(56 * w, 56 * w + 56)
            q = qkv[rows, 0:128]
            kk = jnp.concatenate([qkv[rows, 128:256], zero8], 0)
            vv = jnp.concatenate([qkv[rows, 256:384], zero8], 0)
            qs = jnp.concatenate([jnp.where(low, q, 0.0), jnp.where(low, 0.0, q)], 0).astype(BF16)
            ks = jnp.concatenate([jnp.where(even, kk, 0.0), jnp.where(even, 0.0, kk)], 0)
            vs = jnp.concatenate([jnp.where(even, vv, 0.0), jnp.where(even, 0.0, vv)], 0)
            values.append(vs.astype(BF16))
            scores.append(
                lax.dot_general(
                    qs, ks.astype(BF16), (((1,), (1,)), ((), ())), preferred_element_type=F32
                )
            )
        probs = []
        for w in range(count):
            c = src_cols[w]
            li = labels[pl.ds(lab_row, 7), c : c + 8, :].reshape(56, 128)
            li = jnp.where(pad, -1.0, li)
            lj = jnp.sum(jnp.where(diag, li, 0.0), 0, keepdims=True)
            same = li == lj
            ps = []
            for half in range(2):
                at = slice(128 * half, 128 * half + 128)
                sh = scores[w][56 * half : 56 * half + 56]
                sh = jnp.where(same, sh + bias_ref[block, :, at], NEG)
                m0 = jnp.max(jnp.where(low, sh, NEG), -1, keepdims=True)
                m1 = jnp.max(jnp.where(low, NEG, sh), -1, keepdims=True)
                ps.append(jnp.exp2((sh - jnp.where(low, m0, m1)) * EXPS))
            probs.append(ps)
        sums = dot(
            jnp.concatenate([jnp.concatenate(ps, 1) for ps in probs], 0).astype(BF16), hst
        )
        outs = []
        for w in range(count):
            o = dot(jnp.concatenate(probs[w], 0).astype(BF16), values[w])
            outs.append(jnp.where(low, o[0:56], o[56:112]))
        mixed = (jnp.concatenate(outs, 0) / sums).astype(BF16)
        res = x + dot(mixed, proj_ref[block])
        for w in range(count):
            c = dst_cols[w]
            dst[pl.ds(dst_row, 7), c : c + 8, :] = res[56 * w : 56 * w + 56].reshape(
                7, 8, 128
            )

    def feed(block, h):
        y = norm(h, gains_ref[2 + 2 * block : 3 + 2 * block, :]).astype(BF16)
        u = gelu(dot(y, fc1_ref[block])).astype(BF16)
        return h + dot(u, fc2_ref[block])

    def block0(a, _):
        for g in range(0, wins0, 6):
            cols = [5 + 7 * w for w in range(g, min(g + 6, wins0))]
            attend(0, t0, 7 * a + 1, cols, 7 * a, h1, 7 * a, cols)
        return 0

    lax.fori_loop(0, brows // WIN, block0, 0)

    span = tcols + 8

    def feed0(i, _):
        r = 3 + 7 * i
        h = h1[pl.ds(r, 7), 8 : 8 + span, :].reshape(7 * span, 128)
        t = feed(0, h).astype(BF16).astype(F32)
        h1[pl.ds(r, 7), 8 : 8 + span, :] = t.reshape(7, span, 128)
        return 0

    lax.fori_loop(0, (trows + WIN) // 7, feed0, 0)

    def block1(a, _):
        for g in range(0, wins1, 6):
            ws = range(g, min(g + 6, wins1))
            attend(
                1,
                h1,
                3 + 7 * a,
                [8 + 7 * w for w in ws],
                3 + 7 * a,
                h2,
                7 * a,
                [4 + 7 * w for w in ws],
            )
        return 0

    lax.fori_loop(0, trows // WIN + 1, block1, 0)

    def feed1(i, _):
        r = 7 * i
        h = h2[pl.ds(4 + r, 7), 8 : 8 + tcols, :].reshape(7 * tcols, 128)
        out_ref[pl.ds(r, 7)] = feed(1, h).astype(BF16).reshape(7, tcols, 128)
        return 0

    lax.fori_loop(0, trows // 7, feed1, 0)


def prepare(
    pattern_ref,
    _,
    stem_ref,
    layer0_ref,
    layer1_ref,
    layer2_ref,
    layer3_ref,
    embed_ref,
    table_ref,
    wst_ref,
    wl_ref,
    e2_ref,
    bias_ref,
    across,
):
    zero = jnp.zeros((C, C), F32)
    for layer, taps_ref in enumerate((layer0_ref, layer1_ref, layer2_ref, layer3_ref)):
        blocks = []
        for b in range(3):
            k0, k1, k2 = [taps_ref[0, 0, 3 * a + b].astype(F32) for a in range(3)]
            blocks.append(jnp.concatenate([k1, k2, zero, k0], 1))
            blocks.append(jnp.concatenate([k0, k1, k2, zero], 1))
        wl_ref[layer] = jnp.concatenate(blocks, 0).T.astype(BF16)

    pattern = pattern_ref[0]
    outer = jnp.logical_or(pattern == 0, pattern == 3)
    channel = lax.broadcasted_iota(jnp.int32, (4, 32), 0)
    lane = lax.broadcasted_iota(jnp.int32, (4, 32), 1)
    plane = jnp.where(
        channel == 0,
        pattern,
        jnp.where(
            channel == 1,
            jnp.where(outer, 1, 0),
            jnp.where(channel == 2, jnp.where(outer, 2, 3), 3 - pattern),
        ),
    )
    blocks = []
    for b in range(3):
        for p in range(2):
            total = jnp.zeros((C, 32), F32)
            for a in range(3):
                spread = (lane == 8 * plane + a + p).astype(BF16)
                total = total + dot(stem_ref[0, 3 * a + b], spread)
            blocks.append(total)
    wst_ref[...] = jnp.concatenate(blocks, 0).T.astype(BF16)

    embed = embed_ref[...]
    blank = jnp.zeros_like(embed)
    e2_ref[...] = jnp.concatenate(
        [jnp.concatenate([embed, blank], 1), jnp.concatenate([blank, embed], 1)], 0
    )

    table = table_ref[...] * HD**0.5
    part0 = table.astype(BF16)
    part1 = (table - part0.astype(F32)).astype(BF16)
    part2 = (table - part0.astype(F32) - part1.astype(F32)).astype(BF16)
    entry = lax.broadcasted_iota(jnp.int32, (table.shape[1], 128), 0)
    spot = lax.broadcasted_iota(jnp.int32, (table.shape[1], 128), 1)
    base = (12 - lax.shift_right_logical(spot, 3)) * 13 + 6 - (spot & 7)
    for c in range(8):
        pick = (entry == base + min(c, 6)).astype(BF16)
        across[c] = dot(part0, pick) + dot(part1, pick) + dot(part2, pick)
    low = lax.broadcasted_iota(jnp.int32, (1, 128), 1) < 64
    for block in range(2):
        for half in range(2):
            at = 4 * block + 2 * half
            g0 = across[:, at, :]
            g1 = across[:, at + 1, :]
            for r in range(7):
                back = (6 - r) * 8
                bias_ref[block, 8 * r : 8 * r + 8, 128 * half : 128 * half + 128] = jnp.where(
                    low, pltpu.roll(g0, (128 - back) % 128, 1), pltpu.roll(g1, (192 - back) % 128, 1)
                )


def prepared(pattern, candidate, stem_bank, layer_bank, embed_weight, rel_table):
    taps = [
        pl.BlockSpec((1, 1, 9, C, C), lambda i, p, c, n=n: (n, c[n + 1], 0, 0, 0))
        for n in range(LAYERS - 1)
    ]
    return pl.pallas_call(
        prepare,
        out_shape=[
            jax.ShapeDtypeStruct((32, 6 * C), BF16),
            jax.ShapeDtypeStruct((LAYERS - 1, 4 * C, 6 * C), BF16),
            jax.ShapeDtypeStruct((2 * C, 2 * D), BF16),
            jax.ShapeDtypeStruct((2, 56, HEADS * 64), F32),
        ],
        grid_spec=pltpu.PrefetchScalarGridSpec(
            num_scalar_prefetch=2,
            grid=(1,),
            in_specs=[pl.BlockSpec((1, 9, C, 4), lambda i, p, c: (c[0], 0, 0, 0))]
            + taps
            + [
                pl.BlockSpec((C, D), lambda i, p, c: (0, 0)),
                pl.BlockSpec((8, 169), lambda i, p, c: (0, 0)),
            ],
            out_specs=[
                pl.BlockSpec((32, 6 * C), lambda i, p, c: (0, 0)),
                pl.BlockSpec((LAYERS - 1, 4 * C, 6 * C), lambda i, p, c: (0, 0, 0)),
                pl.BlockSpec((2 * C, 2 * D), lambda i, p, c: (0, 0)),
                pl.BlockSpec((2, 56, HEADS * 64), lambda i, p, c: (0, 0, 0)),
            ],
            scratch_shapes=[pltpu.VMEM((8, 8, 128), F32)],
        ),
        compiler_params=pltpu.CompilerParams(vmem_limit_bytes=32 * 1024 * 1024),
        cost_estimate=pl.CostEstimate(
            flops=100_000_000, bytes_accessed=4_000_000, transcendentals=0
        ),
    )(
        pattern,
        candidate,
        stem_bank,
        layer_bank,
        layer_bank,
        layer_bank,
        layer_bank,
        embed_weight,
        rel_table.reshape(8, 169),
    )


def swaps(values, axis):
    size = lax.axis_size(axis)
    even = [(i, i ^ 1) for i in range(size)]
    odd = []
    for i in range(1, size - 1, 2):
        odd += [(i, i + 1), (i + 1, i)]
    first = lax.ppermute(values, axis, even)
    second = lax.ppermute(values, axis, odd)
    is_even = lax.axis_index(axis) % 2 == 0
    return jnp.where(is_even, second, first), jnp.where(is_even, first, second)


def computed(sizes, *arrays):
    trows, tcols = sizes[:2]
    frows, fcols = trows + 2 * RIM, tcols + 2 * RIM + 8
    pairs = frows // 2
    brows = trows + 2 * WIN
    vmem = pl.BlockSpec(memory_space=pltpu.VMEM)
    return pl.pallas_call(
        functools.partial(kernel, *sizes),
        out_shape=jax.ShapeDtypeStruct((trows, tcols, D), BF16),
        in_specs=[pl.BlockSpec(memory_space=pltpu.SMEM)] + [vmem] * 10,
        out_specs=vmem,
        scratch_shapes=[
            pltpu.VMEM((4, 8 + frows + 10, fcols), F32),
            pltpu.VMEM((pairs + 1, fcols, 128), F32),
            pltpu.VMEM((pairs + 2, fcols, 128), BF16),
            pltpu.VMEM((pairs + 2, fcols, 128), BF16),
            pltpu.VMEM((fcols, 128), F32),
            pltpu.VMEM((brows, fcols + 8, 128), F32),
            pltpu.VMEM((brows + 2, fcols + 8, 128), F32),
            pltpu.VMEM((brows, fcols + 8, 128), F32),
            pltpu.VMEM((trows + WIN, fcols, 128), F32),
        ],
        compiler_params=pltpu.CompilerParams(vmem_limit_bytes=56 * 1024 * 1024),
    )(*arrays)


def shards(
    planes,
    pattern,
    candidate,
    stem_bank,
    layer_bank,
    embed_weight,
    norm_gains,
    qkv_weight,
    proj_weight,
    rel_table,
    fc1_weight,
    fc2_weight,
    labels,
):
    trows, tcols = labels.shape
    nrows, ncols = lax.axis_size("row"), lax.axis_size("col")
    own = jnp.concatenate([planes, labels.astype(BF16)[None]], 0)
    above, below = swaps(own, "row")
    tall = jnp.concatenate([above[:, trows - RIM :], own, below[:, :RIM]], 1)
    ends = jnp.concatenate([tall[:, :, :RIM], tall[:, :, tcols - RIM :]], 2)
    left, right = swaps(ends, "col")
    blank = jnp.zeros((5, trows + 2 * RIM, 8), BF16)
    wide = jnp.concatenate([left[:, :, RIM:], tall, right[:, :, :RIM], blank], 2)

    wst, wl, e2, bias = prepared(
        pattern, candidate, stem_bank, layer_bank, embed_weight, rel_table
    )
    place = jnp.stack([lax.axis_index("row"), lax.axis_index("col")]).astype(jnp.int32)

    return computed(
        (trows, tcols, nrows, ncols),
        place,
        wide,
        wst,
        wl,
        e2,
        norm_gains,
        qkv_weight,
        proj_weight,
        bias,
        fc1_weight,
        fc2_weight,
    )


def solution(mesh):
    placed = (
        P(None, "row", "col"),
        P(),
        P(),
        P(),
        P(),
        P(),
        P(),
        P(),
        P(),
        P(),
        P(),
        P(),
        P("row", "col"),
    )
    return jax.shard_map(
        shards, mesh=mesh, in_specs=placed, out_specs=P("row", "col", None), check_vma=False
    )
```

profile of v0, /device:TPU:160, one launch (start us, length us, event | category | flops | bytes accessed | tf_op | source)
XLA Modules:
  0.0 58.5 jit_solution(3414888700707922576)
XLA Ops:
  0.0 0.7 %convert_bitcast_fusion = bf16[1,14,112]{2,1,0:T(8,128)(2,1)S(1)} fusion(s32[14,112]{1,0:T(8,128)} %param.25), kind=kLoop, calls=%fused_computation.8 | loop fusion | flops 1568 | bytes 9408 | tf_op jit(solution)/shard_map/broadcast_in_dim | solution.py:462
  0.7 0.7 %copy.14 = bf16[4,14,112]{2,1,0:T(8,128)(2,1)S(1)} copy(bf16[4,14,112]{2,0,1:T(4,128)(2,1)} %param.13) | data formatting | bytes 25088 | tf_op args[0]
  1.4 0.1 collective-permute-start.1
  1.5 4.7 %collective-permute-start = (bf16[5,14,112]{2,1,0:T(8,128)(2,1)S(1)}, bf16[5,14,112]{2,1,0:T(8,128)(2,1)S(1)}, u32[]{:S(2)}, u32[]{:S(2)}) collective-permute-start(bf16[5,14,112]{2,1,0:T(8,128)(2,1)S(1)} %pad_maximum_fusion.2), channel_id=1, source_target_pairs={{8,16},{16,8},{24,32},{32,24},{40,48},{48,40},{56,64},{64,56},{72,... | collective-permute-start | bytes 47048 | tf_op jit(solution)/shard_map/ppermute | solution.py:414
  6.3 0.6 %pad_add_fusion.place_ref = s32[2]{0:T(128)} fusion(s32[1]{0:T(128)} %bitcast.1, s32[1]{0:T(128)} %bitcast), kind=kLoop, calls=%fused_computation.9 | loop fusion | flops 2 | bytes 16 | tf_op jit(solution)/shard_map/stack | solution.py:473
  7.5 0.7 %reshape.3.table_ref = f32[8,169]{1,0:T(8,128)S(1)} reshape(f32[2,4,169]{2,1,0:T(4,128)} %param.22) | data formatting | bytes 10816 | tf_op jit(solution)/shard_map/reshape | solution.py:403
  8.2 1.1 %copy.15.stem_ref = bf16[4,9,64,4]{3,2,1,0:T(8,128)(2,1)S(1)} copy(bf16[4,9,64,4]{2,3,1,0:T(4,128)(2,1)} %param.16) | data formatting | bytes 36864 | tf_op args[3]
  9.4 0.1 pad.6.clone
  9.5 1.4 %collective-permute-done = bf16[5,14,112]{2,1,0:T(8,128)(2,1)S(1)} collective-permute-done((bf16[5,14,112]{2,1,0:T(8,128)(2,1)S(1)}, bf16[5,14,112]{2,1,0:T(8,128)(2,1)S(1)}, u32[]{:S(2)}, u32[]{:S(2)}) %collective-permute-start) | collective-permute-done | bytes 15712 | tf_op jit(solution)/shard_map/ppermute | solution.py:414
  10.9 0.1 fusion
  11.0 0.1 pad_maximum_fusion.1
  11.1 1.7 %collective-permute-start.3 = (bf16[5,38,24]{2,1,0:T(8,128)(2,1)S(1)}, bf16[5,38,24]{2,1,0:T(8,128)(2,1)S(1)}, u32[]{:S(2)}, u32[]{:S(2)}) collective-permute-start(bf16[5,38,24]{2,1,0:T(8,128)(2,1)S(1)} %pad_maximum_fusion.1), channel_id=1, source_target_pairs={{0,1},{1,0},{2,3},{3,2},{4,5},{5,4},{6,7},{7,6},{8,9},{9,8},{10,11... | collective-permute-start | bytes 27368 | tf_op jit(solution)/shard_map/ppermute | solution.py:413
  12.8 4.5 %collective-permute-start.2 = (bf16[5,38,24]{2,1,0:T(8,128)(2,1)S(1)}, bf16[5,38,24]{2,1,0:T(8,128)(2,1)S(1)}, u32[]{:S(2)}, u32[]{:S(2)}) collective-permute-start(bf16[5,38,24]{2,1,0:T(8,128)(2,1)S(1)} %pad_maximum_fusion.1), channel_id=1, source_target_pairs={{1,2},{2,1},{3,4},{4,3},{5,6},{6,5},{9,10},{10,9},{11,12},{12,11},... | collective-permute-start | bytes 27368 | tf_op jit(solution)/shard_map/ppermute | solution.py:414
  17.3 1.7 %copy-done = bf16[4,4,9,64,64]{4,3,2,1,0:T(8,128)(2,1)S(1)} copy-done((bf16[4,4,9,64,64]{4,3,2,1,0:T(8,128)(2,1)S(1)}, bf16[4,4,9,64,64]{4,3,2,1,0:T(8,128)(2,1)}, u32[]{:S(2)}) %copy-start) | copy-done | bytes 1179672
  19.0 0.7 %copy-done.5 = bf16[64,128]{1,0:T(8,128)(2,1)S(1)} copy-done((bf16[64,128]{1,0:T(8,128)(2,1)S(1)}, bf16[64,128]{1,0:T(8,128)(2,1)}, u32[]{:S(2)}) %copy-start.5) | copy-done | bytes 16408
  19.7 0.7 %copy-done.6 = s32[5]{0:T(128)S(1)} copy-done((s32[5]{0:T(128)S(1)}, s32[5]{0:T(128)}, u32[]{:S(2)}) %copy-start.6) | copy-done | bytes 44
  20.3 1.2 %shard_map.127 = (bf16[32,384]{1,0:T(8,128)(2,1)S(1)}, bf16[4,256,384]{2,1,0:T(8,128)(2,1)S(1)}, bf16[128,256]{1,0:T(8,128)(2,1)S(1)}, f32[2,56,256]{2,1,0:T(8,128)S(1)}) custom-call(s32[1]{0:T(128)S(6)} %copy.16.pattern_ref, s32[5]{0:T(128)S(1)} %copy-done.6, bf16[4,9,64,4]{3,2,1,0:T(8,128)(2,1)S(1)} %copy.15.stem_ref, ...), custom_call_target="tpu_custom_call" | custom-call | flops 100000000 | bytes 4000000 | tf_op jit(solution)/shard_map/pallas_call | solution.py:365
  21.5 0.9 %copy-done.1 = bf16[4,256,384]{2,1,0:T(8,128)(2,1)} copy-done((bf16[4,256,384]{2,1,0:T(8,128)(2,1)}, bf16[4,256,384]{2,1,0:T(8,128)(2,1)S(1)}, u32[]{:S(2)}) %copy-start.1) | copy-done | bytes 786456
  22.5 0.6 %copy-done.2 = f32[2,56,256]{2,1,0:T(8,128)} copy-done((f32[2,56,256]{2,1,0:T(8,128)}, f32[2,56,256]{2,1,0:T(8,128)S(1)}, u32[]{:S(2)}) %copy-start.2) | copy-done | bytes 114712
  23.1 0.6 %copy-done.3 = bf16[128,256]{1,0:T(8,128)(2,1)} copy-done((bf16[128,256]{1,0:T(8,128)(2,1)}, bf16[128,256]{1,0:T(8,128)(2,1)S(1)}, u32[]{:S(2)}) %copy-start.3) | copy-done | bytes 65560
  23.7 0.6 %copy-done.4 = bf16[32,384]{1,0:T(8,128)(2,1)} copy-done((bf16[32,384]{1,0:T(8,128)(2,1)}, bf16[32,384]{1,0:T(8,128)(2,1)S(1)}, u32[]{:S(2)}) %copy-start.4) | copy-done | bytes 24600
  24.3 0.1 slice_select_fusion.1
  24.4 0.8 %maximum_maximum_fusion.planes_ref = bf16[5,38,144]{2,1,0:T(8,128)(2,1)} fusion(bf16[5,38,12]{2,1,0:T(8,128)(2,1)S(1)} %get-tuple-element.14, bf16[5,12,112]{2,1,0:T(8,128)(2,1)S(1)} %get-tuple-element.18, bf16[1,14,112]{2,1,0:T(8,128)(2,1)S(1)} %convert_bitcast_fusion, bf16[4,14,112]{2,1,0:T(8,128)(2,1)S(1)} %copy.14, ...), kind=kLoop, calls=%fused_computation | loop fusion | flops 383040 | bytes 106688 | tf_op jit(solution)/shard_map/concatenate | solution.py:468
  25.2 33.3 %shard_map.128 = bf16[14,112,128]{2,1,0:T(8,128)(2,1)} custom-call(s32[2]{0:T(128)} %pad_add_fusion.place_ref, bf16[5,38,144]{2,1,0:T(8,128)(2,1)} %maximum_maximum_fusion.planes_ref, bf16[32,384]{1,0:T(8,128)(2,1)} %copy-done.4, bf16[4,256,384]{2,1,0:T(8,128)(2,1)} %copy-done.1, bf16[128,256]{1,0:T(8,128)(2,1)} %copy-done.3, f32[5,128]{1,0:T(8,128)} %gains_ref.1, ...), custom_call_target="tpu_custom_call" | custom-call | tf_op jit(solution)/shard_map/pallas_call | solution.py:425
  (14 shorter events, 0.1 us)
Async XLA Ops:
  1.4 8.0 %collective-permute-start.1 = (bf16[5,14,112]{2,1,0:T(8,128)(2,1)S(1)}, bf16[5,14,112]{2,1,0:T(8,128)(2,1)S(1)}, u32[]{:S(2)}, u32[]{:S(2)}) collective-permute-start(bf16[5,14,112]{2,1,0:T(8,128)(2,1)S(1)} %pad_maximum_fusion.2), channel_id=1, source_target_pairs={{0,8},{8,0},{16,24},{24,16},{32,40},{40,32},{48,56},{56,48},{64,72... | collective-permute-start | bytes 47048 | tf_op jit(solution)/shard_map/ppermute | solution.py:413
  1.5 9.3 %collective-permute-start = (bf16[5,14,112]{2,1,0:T(8,128)(2,1)S(1)}, bf16[5,14,112]{2,1,0:T(8,128)(2,1)S(1)}, u32[]{:S(2)}, u32[]{:S(2)}) collective-permute-start(bf16[5,14,112]{2,1,0:T(8,128)(2,1)S(1)} %pad_maximum_fusion.2), channel_id=1, source_target_pairs={{8,16},{16,8},{24,32},{32,24},{40,48},{48,40},{56,64},{64,56},{72,... | collective-permute-start | bytes 47048 | tf_op jit(solution)/shard_map/ppermute | solution.py:414
  11.1 13.2 %collective-permute-start.3 = (bf16[5,38,24]{2,1,0:T(8,128)(2,1)S(1)}, bf16[5,38,24]{2,1,0:T(8,128)(2,1)S(1)}, u32[]{:S(2)}, u32[]{:S(2)}) collective-permute-start(bf16[5,38,24]{2,1,0:T(8,128)(2,1)S(1)} %pad_maximum_fusion.1), channel_id=1, source_target_pairs={{0,1},{1,0},{2,3},{3,2},{4,5},{5,4},{6,7},{7,6},{8,9},{9,8},{10,11... | collective-permute-start | bytes 27368 | tf_op jit(solution)/shard_map/ppermute | solution.py:413
  12.8 11.6 %collective-permute-start.2 = (bf16[5,38,24]{2,1,0:T(8,128)(2,1)S(1)}, bf16[5,38,24]{2,1,0:T(8,128)(2,1)S(1)}, u32[]{:S(2)}, u32[]{:S(2)}) collective-permute-start(bf16[5,38,24]{2,1,0:T(8,128)(2,1)S(1)} %pad_maximum_fusion.1), channel_id=1, source_target_pairs={{1,2},{2,1},{3,4},{4,3},{5,6},{6,5},{9,10},{10,9},{11,12},{12,11},... | collective-permute-start | bytes 27368 | tf_op jit(solution)/shard_map/ppermute | solution.py:414
  17.3 1.7 %copy-start = (bf16[4,4,9,64,64]{4,3,2,1,0:T(8,128)(2,1)S(1)}, bf16[4,4,9,64,64]{4,3,2,1,0:T(8,128)(2,1)}, u32[]{:S(2)}) copy-start(bf16[4,4,9,64,64]{4,3,2,1,0:T(8,128)(2,1)} %layer3_ref.1) | copy-start | bytes 3538948
  18.9 0.7 %copy-start.5 = (bf16[64,128]{1,0:T(8,128)(2,1)S(1)}, bf16[64,128]{1,0:T(8,128)(2,1)}, u32[]{:S(2)}) copy-start(bf16[64,128]{1,0:T(8,128)(2,1)} %embed_ref.1) | copy-start | bytes 49156
  19.7 0.7 %copy-start.6 = (s32[5]{0:T(128)S(1)}, s32[5]{0:T(128)}, u32[]{:S(2)}) copy-start(s32[5]{0:T(128)} %_.1) | copy-start | bytes 64
  21.5 0.9 %copy-start.1 = (bf16[4,256,384]{2,1,0:T(8,128)(2,1)}, bf16[4,256,384]{2,1,0:T(8,128)(2,1)S(1)}, u32[]{:S(2)}) copy-start(bf16[4,256,384]{2,1,0:T(8,128)(2,1)S(1)} %get-tuple-element.10.wl_ref) | copy-start | bytes 2359300
  22.4 0.6 %copy-start.2 = (f32[2,56,256]{2,1,0:T(8,128)}, f32[2,56,256]{2,1,0:T(8,128)S(1)}, u32[]{:S(2)}) copy-start(f32[2,56,256]{2,1,0:T(8,128)S(1)} %get-tuple-element.12.bias_ref) | copy-start | bytes 344068
  23.1 0.6 %copy-start.3 = (bf16[128,256]{1,0:T(8,128)(2,1)}, bf16[128,256]{1,0:T(8,128)(2,1)S(1)}, u32[]{:S(2)}) copy-start(bf16[128,256]{1,0:T(8,128)(2,1)S(1)} %get-tuple-element.11.e2_ref) | copy-start | bytes 196612
  23.7 0.6 %copy-start.4 = (bf16[32,384]{1,0:T(8,128)(2,1)}, bf16[32,384]{1,0:T(8,128)(2,1)S(1)}, u32[]{:S(2)}) copy-start(bf16[32,384]{1,0:T(8,128)(2,1)S(1)} %get-tuple-element.9.wst_ref) | copy-start | bytes 73732
where the time goes:
time: 59 us; the launch traced here: 58.5 us
  Pallas kernels  34.5 us (58%)
  starting transfers between devices  11 us (19%)
  local copies, waits for them, and re-layouts  8.52 us (14%)
  other arithmetic  2.32 us (4%)
  waiting for transfers between devices  1.4 us (2%)
  between operations  0.75 us (1%)
    pallas_call x1, Pallas kernels, computed(): pl.pallas_call(functools.partial(kernel, *sizes), out_shape=jax.ShapeDtyp...  33.3 us
    ppermute x2, starting transfers between devices, swaps(): second = lax.ppermute(values, axis, odd)  9.27 us
    unnamed x16, local copies, waits for them, and re-layouts  7.65 us
    ppermute x2, starting transfers between devices, swaps(): first = lax.ppermute(values, axis, even)  1.76 us
    ppermute x2, waiting for transfers between devices, swaps(): second = lax.ppermute(values, axis, odd)  1.4 us
    pallas_call x1, Pallas kernels, prepared(): pl.pallas_call(prepare, out_shape=[jax.ShapeDtypeStruct((32, 6 * C), BF16...  1.2 us
  transfers between devices with their start and end apart: 4, of which 1 were waited for; matrix products, arithmetic and copies ran while one was open for 4% of the time, Pallas kernels for 2%

commit v1 on v0

--- a/solution.py
+++ b/solution.py
@@ -20,14 +20,19 @@
 F32 = jnp.float32
 BF16 = jnp.bfloat16
 NEG = -1e30
-EXPS = HD ** (-0.5) * 1.4426950408889634
+LOG2E = 1.4426950408889634
+ROOT_HALF = 0.7071067811865476
+LIMIT = 1e25
+VMEM = 60 * 1024 * 1024
+
+
+def scaled(centred, scales):
+    total = jnp.sum(centred * centred, -1, keepdims=True)
+    return centred * lax.rsqrt(total + D * EPSILON) * (scales * D**0.5)
 
 
 def norm(values, scales):
-    centre = jnp.mean(values, -1, keepdims=True)
-    centred = values - centre
-    spread = jnp.mean(centred * centred, -1, keepdims=True)
-    return centred * lax.rsqrt(spread + EPSILON) * scales
+    return scaled(values - jnp.mean(values, -1, keepdims=True), scales)
 
 
 def dot(a, b):
@@ -37,10 +42,6 @@
 def silu(v):
     half = 0.5 * v
     return half + half * jnp.tanh(half)
-
-
-def gelu(v):
-    return 0.5 * v * (1.0 + lax.erf(v * 0.7071067811865476))
 
 
 def kernel(
@@ -49,17 +50,26 @@
     nrows,
     ncols,
     place_ref,
-    planes_ref,
+    tall_ref,
+    left_ref,
+    right_ref,
     wst_ref,
-    wl_ref,
     e2_ref,
     gains_ref,
+    wl_hbm,
+    qkv_hbm,
+    proj_hbm,
+    bias_hbm,
+    fc1_hbm,
+    fc2_hbm,
+    out_ref,
+    wl_ref,
     qkv_ref,
     proj_ref,
     bias_ref,
     fc1_ref,
     fc2_ref,
-    out_ref,
+    sems,
     raw,
     state,
     act_a,
@@ -69,6 +79,7 @@
     t0,
     h1,
     h2,
+    check,
 ):
     frows = trows + 2 * RIM
     fcols = tcols + 2 * RIM + 8
@@ -82,20 +93,36 @@
     lane = lax.broadcasted_iota(jnp.int32, (1, 128), 1)
     low = lane < C
 
+    sources = (wl_hbm, qkv_hbm, bias_hbm, proj_hbm, fc1_hbm, fc2_hbm)
+    targets = (wl_ref, qkv_ref, bias_ref, proj_ref, fc1_ref, fc2_ref)
+    copies = [
+        pltpu.make_async_copy(source, target, sems.at[n])
+        for n, (source, target) in enumerate(zip(sources, targets))
+    ]
+    for copy in copies:
+        copy.start()
+
     raw[...] = jnp.zeros_like(raw)
-    for c in range(4):
-        raw[c, 8 : 8 + frows, :] = planes_ref[c].astype(F32)
+    mine = jnp.concatenate(
+        [
+            left_ref[...].astype(F32)[:, :, RIM:],
+            tall_ref[...].astype(F32),
+            right_ref[...].astype(F32)[:, :, :RIM],
+            jnp.zeros((frows, 5, 8), F32),
+        ],
+        2,
+    )
+    grow = lax.broadcasted_iota(jnp.int32, mine.shape, 0) + row_at
+    gcol = lax.broadcasted_iota(jnp.int32, mine.shape, 2) + col_at
+    inside = (grow >= 0) & (grow < nrows * trows) & (gcol >= 0) & (gcol < ncols * tcols)
+    raw[1 : 1 + frows, 0:5, :] = jnp.where(inside, mine, 0.0)
     act_a[0] = jnp.zeros_like(act_a[0])
     act_b[0] = jnp.zeros_like(act_b[0])
+    act_b[1] = jnp.zeros_like(act_b[0])
     act_a[pairs + 1] = jnp.zeros_like(act_a[0])
     act_b[pairs + 1] = jnp.zeros_like(act_b[0])
     gcol = lax.broadcasted_iota(jnp.int32, (fcols, 128), 0) + col_at
     colmask[...] = ((gcol >= 0) & (gcol < ncols * tcols)).astype(F32)
-
-    lab = planes_ref[4].astype(F32) + 1.0
-    lab = jnp.concatenate([lab, jnp.zeros((2, fcols), F32)], 0).T
-    for r in range(brows):
-        labels[r, 0:fcols, :] = jnp.broadcast_to(lab[:, 5 + r : 6 + r], (fcols, 128))
 
     def rowmask(k):
         g = row_at + 2 * k
@@ -114,19 +141,21 @@
         return (silu(x) * (colmask[...] * rowmask(k))).astype(BF16)
 
     def stem(g, _):
-        rows = [raw[c, pl.ds(pl.multiple_of(8 * g, 8), 24), :] for c in range(4)]
-        for i in range(4):
-            k = 4 * g + i
-            lhs = jnp.concatenate([v[2 * i + 7 : 2 * i + 15] for v in rows], 0).astype(BF16)
+        for i in range(5):
+            k = 5 * g + i
+            lhs = raw[pl.ds(2 * k, 4)].reshape(32, fcols).astype(BF16)
             y = lax.dot_general(
                 lhs, wst_ref[...], (((0,), (0,)), ((), ())), preferred_element_type=F32
             )
             x = gathered(y)
             state[k] = x
             act_a[k + 1] = act_of(x, k)
+            labels[2 * k, 0:fcols, :] = y[:, 384:512]
+            labels[2 * k + 1, 0:fcols, :] = y[:, 512:640]
         return 0
 
-    lax.fori_loop(0, (pairs + 3) // 4, stem, 0)
+    lax.fori_loop(0, (pairs + 1) // 5, stem, 0)
+    copies[0].wait()
 
     spans = [(1, pairs, 6), (1, pairs, 6), (2, pairs - 2, 5), (2, pairs - 2, 5)]
     bufs = [act_a, act_b]
@@ -156,13 +185,14 @@
                 else:
                     xs.append(x)
             if layer == LAYERS - 2:
-                z = dot(jnp.concatenate(xs, 0).astype(BF16), e2_ref[...])
+                x5 = jnp.concatenate(xs, 0).astype(BF16)
+                z = dot(jnp.concatenate([x5, x5], 1), e2_ref[...])
                 g = gains_ref[0:1, :]
                 for j in range(many):
                     r = 2 * (k0 + j) - 4
                     zz = z[fcols * j : fcols * j + fcols]
-                    t0[r, 0:fcols, :] = norm(zz[:, 0:128], g).astype(BF16).astype(F32)
-                    t0[r + 1, 0:fcols, :] = norm(zz[:, 128:256], g).astype(BF16).astype(F32)
+                    t0[r, 0:fcols, :] = scaled(zz[:, 0:128], g)
+                    t0[r + 1, 0:fcols, :] = scaled(zz[:, 128:256], g)
             return 0
 
         lax.fori_loop(0, (hi - lo) // many, conv, 0)
@@ -177,7 +207,7 @@
     even = (lane & 32) == 0
     zero8 = jnp.zeros((8, 128), F32)
 
-    def attend(block, src, src_row, src_cols, lab_row, dst, dst_row, dst_cols):
+    def attend(block, exact, src, src_row, src_cols, lab_row, dst, dst_row, dst_cols):
         count = len(src_cols)
         x = jnp.concatenate(
             [src[pl.ds(src_row, 7), c : c + 8, :].reshape(56, 128) for c in src_cols], 0
@@ -187,7 +217,7 @@
         scores, values = [], []
         for w in range(count):
             rows = slice(56 * w, 56 * w + 56)
-            q = qkv[rows, 0:128]
+            q = qkv[rows, 0:128] * (LOG2E * HD**-0.5)
             kk = jnp.concatenate([qkv[rows, 128:256], zero8], 0)
             vv = jnp.concatenate([qkv[rows, 256:384], zero8], 0)
             qs = jnp.concatenate([jnp.where(low, q, 0.0), jnp.where(low, 0.0, q)], 0).astype(BF16)
@@ -211,9 +241,11 @@
                 at = slice(128 * half, 128 * half + 128)
                 sh = scores[w][56 * half : 56 * half + 56]
                 sh = jnp.where(same, sh + bias_ref[block, :, at], NEG)
-                m0 = jnp.max(jnp.where(low, sh, NEG), -1, keepdims=True)
-                m1 = jnp.max(jnp.where(low, NEG, sh), -1, keepdims=True)
-                ps.append(jnp.exp2((sh - jnp.where(low, m0, m1)) * EXPS))
+                if exact:
+                    m0 = jnp.max(jnp.where(low, sh, NEG), -1, keepdims=True)
+                    m1 = jnp.max(jnp.where(low, NEG, sh), -1, keepdims=True)
+                    sh = sh - jnp.where(low, m0, m1)
+                ps.append(jnp.exp2(sh))
             probs.append(ps)
         sums = dot(
             jnp.concatenate([jnp.concatenate(ps, 1) for ps in probs], 0).astype(BF16), hst
@@ -222,7 +254,11 @@
         for w in range(count):
             o = dot(jnp.concatenate(probs[w], 0).astype(BF16), values[w])
             outs.append(jnp.where(low, o[0:56], o[56:112]))
-        mixed = (jnp.concatenate(outs, 0) / sums).astype(BF16)
+        over = 1.0 / sums
+        if not exact:
+            worst = jnp.max(jnp.maximum(sums, over).reshape(7 * count, 8, 128), 0)
+            check[...] = jnp.maximum(check[...], worst)
+        mixed = (jnp.concatenate(outs, 0) * over).astype(BF16)
         res = x + dot(mixed, proj_ref[block])
         for w in range(count):
             c = dst_cols[w]
@@ -231,45 +267,51 @@
             )
 
     def feed(block, h):
-        y = norm(h, gains_ref[2 + 2 * block : 3 + 2 * block, :]).astype(BF16)
-        u = gelu(dot(y, fc1_ref[block])).astype(BF16)
-        return h + dot(u, fc2_ref[block])
-
-    def block0(a, _):
+        y = norm(h, gains_ref[2 + 2 * block : 3 + 2 * block, :] * ROOT_HALF).astype(BF16)
+        v = dot(y, fc1_ref[block])
+        u = (v * (1.0 + lax.erf(v))).astype(BF16)
+        return h + dot(u, fc2_ref[block]) * ROOT_HALF
+
+    def blocks(count, groups, block):
+        check[...] = jnp.zeros_like(check)
+        lax.fori_loop(0, count, lambda a, _: groups(a, False, block), 0)
+
+        @pl.when(jnp.logical_not(jnp.max(check[...]) < LIMIT))
+        def _():
+            lax.fori_loop(0, count, lambda a, _: groups(a, True, block), 0)
+
+    def groups0(a, exact, block):
         for g in range(0, wins0, 6):
             cols = [5 + 7 * w for w in range(g, min(g + 6, wins0))]
-            attend(0, t0, 7 * a + 1, cols, 7 * a, h1, 7 * a, cols)
+            attend(block, exact, t0, 7 * a + 1, cols, 7 * a + 5, h1, 7 * a, cols)
         return 0
 
-    lax.fori_loop(0, brows // WIN, block0, 0)
+    for copy in copies[1:4]:
+        copy.wait()
+    blocks(brows // WIN, groups0, 0)
+    for copy in copies[4:6]:
+        copy.wait()
 
     span = tcols + 8
 
     def feed0(i, _):
         r = 3 + 7 * i
         h = h1[pl.ds(r, 7), 8 : 8 + span, :].reshape(7 * span, 128)
-        t = feed(0, h).astype(BF16).astype(F32)
+        t = feed(0, h)
         h1[pl.ds(r, 7), 8 : 8 + span, :] = t.reshape(7, span, 128)
         return 0
 
     lax.fori_loop(0, (trows + WIN) // 7, feed0, 0)
 
-    def block1(a, _):
+    def groups1(a, exact, block):
         for g in range(0, wins1, 6):
             ws = range(g, min(g + 6, wins1))
-            attend(
-                1,
-                h1,
-                3 + 7 * a,
-                [8 + 7 * w for w in ws],
-                3 + 7 * a,
-                h2,
-                7 * a,
-                [4 + 7 * w for w in ws],
-            )
+            from_cols = [8 + 7 * w for w in ws]
+            to_cols = [4 + 7 * w for w in ws]
+            attend(block, exact, h1, 3 + 7 * a, from_cols, 8 + 7 * a, h2, 7 * a, to_cols)
         return 0
 
-    lax.fori_loop(0, trows // WIN + 1, block1, 0)
+    blocks(trows // WIN + 1, groups1, 1)
 
     def feed1(i, _):
         r = 7 * i
@@ -307,8 +349,8 @@
 
     pattern = pattern_ref[0]
     outer = jnp.logical_or(pattern == 0, pattern == 3)
-    channel = lax.broadcasted_iota(jnp.int32, (4, 32), 0)
-    lane = lax.broadcasted_iota(jnp.int32, (4, 32), 1)
+    row = lax.broadcasted_iota(jnp.int32, (32, 16), 0)
+    channel = lax.broadcasted_iota(jnp.int32, (32, 16), 1)
     plane = jnp.where(
         channel == 0,
         pattern,
@@ -318,23 +360,38 @@
             jnp.where(channel == 2, jnp.where(outer, 2, 3), 3 - pattern),
         ),
     )
+    taps = [
+        jnp.concatenate([stem_ref[0, t].astype(F32), jnp.zeros((12, C), F32)], 0).astype(BF16)
+        for t in range(9)
+    ]
     blocks = []
     for b in range(3):
         for p in range(2):
-            total = jnp.zeros((C, 32), F32)
+            total = jnp.zeros((32, C), F32)
             for a in range(3):
-                spread = (lane == 8 * plane + a + p).astype(BF16)
-                total = total + dot(stem_ref[0, 3 * a + b], spread)
+                spread = ((row == 8 * (a + p) + plane) & (channel < 4)).astype(BF16)
+                total = total + dot(spread, taps[3 * a + b])
             blocks.append(total)
-    wst_ref[...] = jnp.concatenate(blocks, 0).T.astype(BF16)
-
-    embed = embed_ref[...]
+    row = lax.broadcasted_iota(jnp.int32, (32, 128), 0)
+    for p in range(2):
+        blocks.append((row == 8 * (1 + p) + 4).astype(F32))
+    wst_ref[...] = jnp.concatenate(blocks, 1).astype(BF16)
+
+    embed = embed_ref[...].astype(F32)
+    embed = embed - jnp.mean(embed, -1, keepdims=True)
+    high = embed.astype(BF16).astype(F32)
     blank = jnp.zeros_like(embed)
     e2_ref[...] = jnp.concatenate(
-        [jnp.concatenate([embed, blank], 1), jnp.concatenate([blank, embed], 1)], 0
-    )
-
-    table = table_ref[...] * HD**0.5
+        [
+            jnp.concatenate(pair, 1)
+            for part in (high, embed - high)
+            for pair in ((part, blank), (blank, part))
+        ],
+        0,
+    ).astype(BF16)
+
+    table = jnp.concatenate([table_ref[0], table_ref[1]], 0) * LOG2E
+    table = jnp.concatenate([table, jnp.zeros((8, 256 - table.shape[1]), F32)], 1)
     part0 = table.astype(BF16)
     part1 = (table - part0.astype(F32)).astype(BF16)
     part2 = (table - part0.astype(F32) - part1.astype(F32)).astype(BF16)
@@ -365,53 +422,55 @@
     return pl.pallas_call(
         prepare,
         out_shape=[
-            jax.ShapeDtypeStruct((32, 6 * C), BF16),
+            jax.ShapeDtypeStruct((32, 6 * C + 2 * D), BF16),
             jax.ShapeDtypeStruct((LAYERS - 1, 4 * C, 6 * C), BF16),
-            jax.ShapeDtypeStruct((2 * C, 2 * D), BF16),
+            jax.ShapeDtypeStruct((4 * C, 2 * D), BF16),
             jax.ShapeDtypeStruct((2, 56, HEADS * 64), F32),
         ],
         grid_spec=pltpu.PrefetchScalarGridSpec(
             num_scalar_prefetch=2,
             grid=(1,),
-            in_specs=[pl.BlockSpec((1, 9, C, 4), lambda i, p, c: (c[0], 0, 0, 0))]
+            in_specs=[pl.BlockSpec((1, 9, 4, C), lambda i, p, c: (c[0], 0, 0, 0))]
             + taps
             + [
                 pl.BlockSpec((C, D), lambda i, p, c: (0, 0)),
-                pl.BlockSpec((8, 169), lambda i, p, c: (0, 0)),
+                pl.BlockSpec((2, 4, 169), lambda i, p, c: (0, 0, 0)),
             ],
             out_specs=[
-                pl.BlockSpec((32, 6 * C), lambda i, p, c: (0, 0)),
+                pl.BlockSpec((32, 6 * C + 2 * D), lambda i, p, c: (0, 0)),
                 pl.BlockSpec((LAYERS - 1, 4 * C, 6 * C), lambda i, p, c: (0, 0, 0)),
-                pl.BlockSpec((2 * C, 2 * D), lambda i, p, c: (0, 0)),
+                pl.BlockSpec((4 * C, 2 * D), lambda i, p, c: (0, 0)),
                 pl.BlockSpec((2, 56, HEADS * 64), lambda i, p, c: (0, 0, 0)),
             ],
             scratch_shapes=[pltpu.VMEM((8, 8, 128), F32)],
         ),
-        compiler_params=pltpu.CompilerParams(vmem_limit_bytes=32 * 1024 * 1024),
+        compiler_params=pltpu.CompilerParams(vmem_limit_bytes=VMEM),
         cost_estimate=pl.CostEstimate(
             flops=100_000_000, bytes_accessed=4_000_000, transcendentals=0
         ),
     )(
         pattern,
         candidate,
-        stem_bank,
+        stem_bank.swapaxes(2, 3),
         layer_bank,
         layer_bank,
         layer_bank,
         layer_bank,
         embed_weight,
-        rel_table.reshape(8, 169),
+        rel_table,
     )
 
 
 def swaps(values, axis):
     size = lax.axis_size(axis)
     even = [(i, i ^ 1) for i in range(size)]
-    odd = []
-    for i in range(1, size - 1, 2):
-        odd += [(i, i + 1), (i + 1, i)]
-    first = lax.ppermute(values, axis, even)
-    second = lax.ppermute(values, axis, odd)
+    odd = [(i, ((i + 1) ^ 1) - 1) for i in range(size)]
+    odd = [(i, j % size) for i, j in odd]
+    return lax.ppermute(values, axis, even), lax.ppermute(values, axis, odd)
+
+
+def ordered(pair, axis):
+    first, second = pair
     is_even = lax.axis_index(axis) % 2 == 0
     return jnp.where(is_even, second, first), jnp.where(is_even, first, second)
 
@@ -425,20 +484,30 @@
     return pl.pallas_call(
         functools.partial(kernel, *sizes),
         out_shape=jax.ShapeDtypeStruct((trows, tcols, D), BF16),
-        in_specs=[pl.BlockSpec(memory_space=pltpu.SMEM)] + [vmem] * 10,
+        in_specs=[pl.BlockSpec(memory_space=pltpu.SMEM)]
+        + [vmem] * 6
+        + [pl.BlockSpec(memory_space=pl.ANY)] * 6,
         out_specs=vmem,
         scratch_shapes=[
-            pltpu.VMEM((4, 8 + frows + 10, fcols), F32),
+            pltpu.VMEM((LAYERS - 1, 4 * C, 6 * C), BF16),
+            pltpu.VMEM((2, D, 3 * D), BF16),
+            pltpu.VMEM((2, D, D), BF16),
+            pltpu.VMEM((2, 56, HEADS * 64), F32),
+            pltpu.VMEM((2, D, 4 * D), BF16),
+            pltpu.VMEM((2, 4 * D, D), BF16),
+            pltpu.SemaphoreType.DMA((6,)),
+            pltpu.VMEM((frows + 6, 8, fcols), F32),
             pltpu.VMEM((pairs + 1, fcols, 128), F32),
             pltpu.VMEM((pairs + 2, fcols, 128), BF16),
             pltpu.VMEM((pairs + 2, fcols, 128), BF16),
             pltpu.VMEM((fcols, 128), F32),
-            pltpu.VMEM((brows, fcols + 8, 128), F32),
+            pltpu.VMEM((frows + 2, fcols + 8, 128), F32),
             pltpu.VMEM((brows + 2, fcols + 8, 128), F32),
             pltpu.VMEM((brows, fcols + 8, 128), F32),
             pltpu.VMEM((trows + WIN, fcols, 128), F32),
+            pltpu.VMEM((8, 128), F32),
         ],
-        compiler_params=pltpu.CompilerParams(vmem_limit_bytes=56 * 1024 * 1024),
+        compiler_params=pltpu.CompilerParams(vmem_limit_bytes=VMEM),
     )(*arrays)
 
 
@@ -459,27 +528,26 @@
 ):
     trows, tcols = labels.shape
     nrows, ncols = lax.axis_size("row"), lax.axis_size("col")
-    own = jnp.concatenate([planes, labels.astype(BF16)[None]], 0)
-    above, below = swaps(own, "row")
-    tall = jnp.concatenate([above[:, trows - RIM :], own, below[:, :RIM]], 1)
+    own = jnp.concatenate([planes.swapaxes(0, 1), labels.astype(BF16)[:, None]], 1)
+    pair = swaps(own, "row")
+    ready = prepared(pattern, candidate, stem_bank, layer_bank, embed_weight, rel_table)
+    pair, (wst, wl, e2, bias) = lax.optimization_barrier((pair, ready))
+    above, below = ordered(pair, "row")
+    tall = jnp.concatenate([above[trows - RIM :], own, below[:RIM]], 0)
     ends = jnp.concatenate([tall[:, :, :RIM], tall[:, :, tcols - RIM :]], 2)
-    left, right = swaps(ends, "col")
-    blank = jnp.zeros((5, trows + 2 * RIM, 8), BF16)
-    wide = jnp.concatenate([left[:, :, RIM:], tall, right[:, :, :RIM], blank], 2)
-
-    wst, wl, e2, bias = prepared(
-        pattern, candidate, stem_bank, layer_bank, embed_weight, rel_table
-    )
+    left, right = ordered(swaps(ends, "col"), "col")
     place = jnp.stack([lax.axis_index("row"), lax.axis_index("col")]).astype(jnp.int32)
 
     return computed(
         (trows, tcols, nrows, ncols),
         place,
-        wide,
+        tall,
+        left,
+        right,
         wst,
-        wl,
         e2,
         norm_gains,
+        wl,
         qkv_weight,
         proj_weight,
         bias,

time: 59 us -> 69.1 us (1.17)
  the two profiles are of different devices: /device:TPU:160 before, /device:TPU:1 now
where the time goes in v1:
time: 69.1 us; the launch traced here: 68.8 us
  Pallas kernels  48.9 us (71%)
  starting transfers between devices  13.3 us (19%)
  other arithmetic  2.91 us (4%)
  waiting for transfers between devices  2.78 us (4%)
  between operations  0.87 us (1%)
    pallas_call x1, Pallas kernels, computed(): pl.pallas_call(functools.partial(kernel, *sizes), out_shape=jax.ShapeDtyp...  45.4 us
    ppermute x4, starting transfers between devices, swaps(): return (lax.ppermute(values, axis, even), lax.ppermute(values, axis, odd))  13.3 us
    pallas_call x1, Pallas kernels, prepared(): pl.pallas_call(prepare, out_shape=[jax.ShapeDtypeStruct((32, 6 * C + 2 *...  3.47 us
    ppermute x4, waiting for transfers between devices, swaps(): return (lax.ppermute(values, axis, even), lax.ppermute(values, axis, odd))  2.78 us
  transfers between devices with their start and end apart: 4, of which 1 were waited for; matrix products, arithmetic and copies ran while one was open for 1% of the time, Pallas kernels for 5%

profile of v1, /device:TPU:1, one launch (start us, length us, event | category | flops | bytes accessed | tf_op | source)
XLA Modules:
  0.0 68.8 jit_solution(1407931813018817325)
XLA Ops:
  0.0 0.7 %convert_bitcast_fusion = bf16[14,1,112]{2,0,1:T(8,128)(2,1)S(1)} fusion(s32[14,112]{1,0:T(8,128)} %param.25), kind=kLoop, calls=%fused_computation.7 | loop fusion | flops 1568 | bytes 9408 | tf_op jit(solution)/shard_map/broadcast_in_dim | solution.py:531
  0.7 0.7 %pad_maximum_fusion.2 = bf16[14,5,112]{2,1,0:T(8,128)(2,1)S(1)} fusion(bf16[14,1,112]{2,1,0:T(2,128)(2,1)S(1)} %copy.20, bf16[14,4,112]{2,1,0:T(4,128)(2,1)} %bitcast.6), kind=kLoop, calls=%fused_computation.4 | loop fusion | flops 31360 | bytes 31360 | tf_op jit(solution)/shard_map/concatenate | solution.py:531
  1.5 2.7 %collective-permute-start.1 = (bf16[14,5,112]{2,1,0:T(8,128)(2,1)S(1)}, bf16[14,5,112]{2,1,0:T(8,128)(2,1)S(1)}, u32[]{:S(2)}, u32[]{:S(2)}) collective-permute-start(bf16[14,5,112]{2,1,0:T(8,128)(2,1)S(1)} %pad_maximum_fusion.2), channel_id=1, source_target_pairs={{0,248},{8,16},{16,8},{24,32},{32,24},{40,48},{48,40},{56,64},{64,... | collective-permute-start | bytes 47048 | tf_op jit(solution)/shard_map/ppermute | solution.py:469
  4.1 6.8 %collective-permute-start = (bf16[14,5,112]{2,1,0:T(8,128)(2,1)S(1)}, bf16[14,5,112]{2,1,0:T(8,128)(2,1)S(1)}, u32[]{:S(2)}, u32[]{:S(2)}) collective-permute-start(bf16[14,5,112]{2,1,0:T(8,128)(2,1)S(1)} %pad_maximum_fusion.2), channel_id=1, source_target_pairs={{0,8},{8,0},{16,24},{24,16},{32,40},{40,32},{48,56},{56,48},{64,72... | collective-permute-start | bytes 47048 | tf_op jit(solution)/shard_map/ppermute | solution.py:469
  11.6 0.0 copy-start.1
  11.6 3.5 %shard_map.127 = (bf16[32,640]{1,0:T(8,128)(2,1)}, bf16[4,256,384]{2,1,0:T(8,128)(2,1)}, bf16[256,256]{1,0:T(8,128)(2,1)}, f32[2,56,256]{2,1,0:T(8,128)}) custom-call(s32[1]{0:T(128)S(6)} %copy.21.pattern_ref, s32[5]{0:T(128)} %_.1, bf16[4,9,4,64]{3,2,1,0:T(4,128)(2,1)} %bitcast.8, bf16[4,4,9,64,64]{4,3,2,1,0:T(8,128)(2,1)} %layer3_ref.1, ...), custom_call_target="tpu_custom_call" | custom-call | flops 100000000 | bytes 4000000 | tf_op jit(solution)/shard_map/pallas_call | solution.py:422
  15.1 0.0 collective-permute-done.1
  15.1 0.0 collective-permute-done
  15.1 0.0 copy-done.1
  15.2 0.0 copy-start
  15.2 0.1 fusion
  15.3 0.1 pad_maximum_fusion.1
  15.4 1.4 %collective-permute-start.3 = (bf16[38,5,24]{2,1,0:T(8,128)(2,1)S(1)}, bf16[38,5,24]{2,1,0:T(8,128)(2,1)S(1)}, u32[]{:S(2)}, u32[]{:S(2)}) collective-permute-start(bf16[38,5,24]{2,1,0:T(8,128)(2,1)S(1)} %pad_maximum_fusion.1), channel_id=1, source_target_pairs={{0,1},{1,0},{2,3},{3,2},{4,5},{5,4},{6,7},{7,6},{8,9},{9,8},{10,11... | collective-permute-start | bytes 27368 | tf_op jit(solution)/shard_map/ppermute | solution.py:469
  16.8 2.4 %collective-permute-start.2 = (bf16[38,5,24]{2,1,0:T(8,128)(2,1)S(1)}, bf16[38,5,24]{2,1,0:T(8,128)(2,1)S(1)}, u32[]{:S(2)}, u32[]{:S(2)}) collective-permute-start(bf16[38,5,24]{2,1,0:T(8,128)(2,1)S(1)} %pad_maximum_fusion.1), channel_id=1, source_target_pairs={{0,7},{1,2},{2,1},{3,4},{4,3},{5,6},{6,5},{7,0},{8,15},{9,10},{10,... | collective-permute-start | bytes 27368 | tf_op jit(solution)/shard_map/ppermute | solution.py:469
  19.1 0.6 pad_add_fusion.place_ref
  19.8 0.0 collective-permute-done.3
  19.8 2.8 %collective-permute-done.2 = bf16[38,5,24]{2,1,0:T(8,128)(2,1)S(1)} collective-permute-done((bf16[38,5,24]{2,1,0:T(8,128)(2,1)S(1)}, bf16[38,5,24]{2,1,0:T(8,128)(2,1)S(1)}, u32[]{:S(2)}, u32[]{:S(2)}) %collective-permute-start.2) | collective-permute-done | bytes 9152 | tf_op jit(solution)/shard_map/ppermute | solution.py:469
  22.6 0.7 broadcast_select_fusion
  23.2 0.0 copy-done
  23.2 45.4 %shard_map.128 = bf16[14,112,128]{2,1,0:T(8,128)(2,1)} custom-call(s32[2]{0:T(128)} %pad_add_fusion.place_ref, bf16[38,5,112]{2,1,0:T(8,128)(2,1)} %copy-done, bf16[38,5,24]{2,1,0:T(8,128)(2,1)} %get-tuple-element.26.left_ref, bf16[38,5,24]{2,1,0:T(8,128)(2,1)} %get-tuple-element.25.right_ref, bf16[32,640]{1,0:T(8,128)(2,1)} %get-tuple-element.21.wst_ref, ...), custom_call_target="tpu_custom_call" | custom-call | tf_op jit(solution)/shard_map/pallas_call | solution.py:484
  (3 shorter events, 0.1 us)
Async XLA Ops:
  1.5 13.7 %collective-permute-start.1 = (bf16[14,5,112]{2,1,0:T(8,128)(2,1)S(1)}, bf16[14,5,112]{2,1,0:T(8,128)(2,1)S(1)}, u32[]{:S(2)}, u32[]{:S(2)}) collective-permute-start(bf16[14,5,112]{2,1,0:T(8,128)(2,1)S(1)} %pad_maximum_fusion.2), channel_id=1, source_target_pairs={{0,248},{8,16},{16,8},{24,32},{32,24},{40,48},{48,40},{56,64},{64,... | collective-permute-start | bytes 47048 | tf_op jit(solution)/shard_map/ppermute | solution.py:469
  4.1 11.0 %collective-permute-start = (bf16[14,5,112]{2,1,0:T(8,128)(2,1)S(1)}, bf16[14,5,112]{2,1,0:T(8,128)(2,1)S(1)}, u32[]{:S(2)}, u32[]{:S(2)}) collective-permute-start(bf16[14,5,112]{2,1,0:T(8,128)(2,1)S(1)} %pad_maximum_fusion.2), channel_id=1, source_target_pairs={{0,8},{8,0},{16,24},{24,16},{32,40},{40,32},{48,56},{56,48},{64,72... | collective-permute-start | bytes 47048 | tf_op jit(solution)/shard_map/ppermute | solution.py:469
  11.6 3.5 %copy-start.1 = (bf16[4,14,112]{2,0,1:T(4,128)(2,1)S(1)}, bf16[4,14,112]{2,0,1:T(4,128)(2,1)}, u32[]{:S(2)}) copy-start(bf16[4,14,112]{2,0,1:T(4,128)(2,1)} %param.13) | copy-start | bytes 37636
  15.2 8.1 %copy-start = (bf16[38,5,112]{2,1,0:T(8,128)(2,1)}, bf16[38,5,112]{2,1,0:T(8,128)(2,1)S(1)}, u32[]{:S(2)}) copy-start(bf16[38,5,112]{2,1,0:T(8,128)(2,1)S(1)} %pad_maximum_fusion.tall_ref) | copy-start | bytes 127684
  15.4 4.4 %collective-permute-start.3 = (bf16[38,5,24]{2,1,0:T(8,128)(2,1)S(1)}, bf16[38,5,24]{2,1,0:T(8,128)(2,1)S(1)}, u32[]{:S(2)}, u32[]{:S(2)}) collective-permute-start(bf16[38,5,24]{2,1,0:T(8,128)(2,1)S(1)} %pad_maximum_fusion.1), channel_id=1, source_target_pairs={{0,1},{1,0},{2,3},{3,2},{4,5},{5,4},{6,7},{7,6},{8,9},{9,8},{10,11... | collective-permute-start | bytes 27368 | tf_op jit(solution)/shard_map/ppermute | solution.py:469
  16.8 5.8 %collective-permute-start.2 = (bf16[38,5,24]{2,1,0:T(8,128)(2,1)S(1)}, bf16[38,5,24]{2,1,0:T(8,128)(2,1)S(1)}, u32[]{:S(2)}, u32[]{:S(2)}) collective-permute-start(bf16[38,5,24]{2,1,0:T(8,128)(2,1)S(1)} %pad_maximum_fusion.1), channel_id=1, source_target_pairs={{0,7},{1,2},{2,1},{3,4},{4,3},{5,6},{6,5},{7,0},{8,15},{9,10},{10,... | collective-permute-start | bytes 27368 | tf_op jit(solution)/shard_map/ppermute | solution.py:469

commit v2 on v1

--- a/solution.py
+++ b/solution.py
@@ -51,8 +51,8 @@
     ncols,
     place_ref,
     tall_ref,
-    left_ref,
-    right_ref,
+    first_ref,
+    second_ref,
     wst_ref,
     e2_ref,
     gains_ref,
@@ -103,11 +103,14 @@
         copy.start()
 
     raw[...] = jnp.zeros_like(raw)
+    even_col = lax.rem(place_ref[1], 2) == 0
+    first = first_ref[...].astype(F32)
+    second = second_ref[...].astype(F32)
     mine = jnp.concatenate(
         [
-            left_ref[...].astype(F32)[:, :, RIM:],
+            jnp.where(even_col, second, first)[:, :, RIM:],
             tall_ref[...].astype(F32),
-            right_ref[...].astype(F32)[:, :, :RIM],
+            jnp.where(even_col, first, second)[:, :, :RIM],
             jnp.zeros((frows, 5, 8), F32),
         ],
         2,
@@ -150,14 +153,16 @@
             x = gathered(y)
             state[k] = x
             act_a[k + 1] = act_of(x, k)
-            labels[2 * k, 0:fcols, :] = y[:, 384:512]
-            labels[2 * k + 1, 0:fcols, :] = y[:, 512:640]
+            both = y[:, 384:512]
+            swapped = pltpu.roll(both, 64, 1)
+            labels[2 * k, 0:fcols, :] = jnp.where(low, both, swapped)
+            labels[2 * k + 1, 0:fcols, :] = jnp.where(low, swapped, both)
         return 0
 
     lax.fori_loop(0, (pairs + 1) // 5, stem, 0)
     copies[0].wait()
 
-    spans = [(1, pairs, 6), (1, pairs, 6), (2, pairs - 2, 5), (2, pairs - 2, 5)]
+    spans = [(1, pairs, 9), (1, pairs, 9), (2, pairs - 2, 15), (2, pairs - 2, 15)]
     bufs = [act_a, act_b]
     for layer in range(LAYERS - 1):
         src, dst = bufs[layer % 2], bufs[(layer + 1) % 2]
@@ -200,10 +205,6 @@
     token = lax.broadcasted_iota(jnp.int32, (56, 128), 0)
     pad = (token & 7) == 7
     diag = (lax.broadcasted_iota(jnp.int32, (56, 128), 1) & 63) == token
-    hm = [((lane >= 32 * h) & (lane < 32 * h + 32)) for h in range(HEADS)]
-    hst = jnp.concatenate(
-        [jnp.broadcast_to(m.astype(F32), (64, 128)) for m in hm], 0
-    ).astype(BF16)
     even = (lane & 32) == 0
     zero8 = jnp.zeros((8, 128), F32)
 
@@ -230,6 +231,8 @@
                 )
             )
         probs = []
+        most = jnp.ones((8, 128), F32)
+        least = jnp.ones((8, 128), F32)
         for w in range(count):
             c = src_cols[w]
             li = labels[pl.ds(lab_row, 7), c : c + 8, :].reshape(56, 128)
@@ -246,19 +249,23 @@
                     m1 = jnp.max(jnp.where(low, NEG, sh), -1, keepdims=True)
                     sh = sh - jnp.where(low, m0, m1)
                 ps.append(jnp.exp2(sh))
+            for half in range(2):
+                l0 = jnp.sum(jnp.where(low, ps[half], 0.0), -1, keepdims=True)
+                l1 = jnp.sum(jnp.where(low, 0.0, ps[half]), -1, keepdims=True)
+                over = 1.0 / jnp.where(low, l0, l1)
+                if not exact:
+                    folded = over.reshape(7, 8, 128)
+                    most = jnp.maximum(most, jnp.max(folded, 0))
+                    least = jnp.minimum(least, jnp.min(folded, 0))
+                ps[half] = ps[half] * over
             probs.append(ps)
-        sums = dot(
-            jnp.concatenate([jnp.concatenate(ps, 1) for ps in probs], 0).astype(BF16), hst
-        )
         outs = []
         for w in range(count):
             o = dot(jnp.concatenate(probs[w], 0).astype(BF16), values[w])
             outs.append(jnp.where(low, o[0:56], o[56:112]))
-        over = 1.0 / sums
         if not exact:
-            worst = jnp.max(jnp.maximum(sums, over).reshape(7 * count, 8, 128), 0)
-            check[...] = jnp.maximum(check[...], worst)
-        mixed = (jnp.concatenate(outs, 0) * over).astype(BF16)
+            check[...] = jnp.maximum(check[...], jnp.maximum(most, 1.0 / least))
+        mixed = jnp.concatenate(outs, 0).astype(BF16)
         res = x + dot(mixed, proj_ref[block])
         for w in range(count):
             c = dst_cols[w]
@@ -281,8 +288,8 @@
             lax.fori_loop(0, count, lambda a, _: groups(a, True, block), 0)
 
     def groups0(a, exact, block):
-        for g in range(0, wins0, 6):
-            cols = [5 + 7 * w for w in range(g, min(g + 6, wins0))]
+        for g in range(0, wins0, 18):
+            cols = [5 + 7 * w for w in range(g, min(g + 18, wins0))]
             attend(block, exact, t0, 7 * a + 1, cols, 7 * a + 5, h1, 7 * a, cols)
         return 0
 
@@ -295,17 +302,17 @@
     span = tcols + 8
 
     def feed0(i, _):
-        r = 3 + 7 * i
-        h = h1[pl.ds(r, 7), 8 : 8 + span, :].reshape(7 * span, 128)
+        r = 3 + 21 * i
+        h = h1[pl.ds(r, 21), 8 : 8 + span, :].reshape(21 * span, 128)
         t = feed(0, h)
-        h1[pl.ds(r, 7), 8 : 8 + span, :] = t.reshape(7, span, 128)
+        h1[pl.ds(r, 21), 8 : 8 + span, :] = t.reshape(21, span, 128)
         return 0
 
-    lax.fori_loop(0, (trows + WIN) // 7, feed0, 0)
+    lax.fori_loop(0, (trows + WIN) // 21, feed0, 0)
 
     def groups1(a, exact, block):
-        for g in range(0, wins1, 6):
-            ws = range(g, min(g + 6, wins1))
+        for g in range(0, wins1, 18):
+            ws = range(g, min(g + 18, wins1))
             from_cols = [8 + 7 * w for w in ws]
             to_cols = [4 + 7 * w for w in ws]
             attend(block, exact, h1, 3 + 7 * a, from_cols, 8 + 7 * a, h2, 7 * a, to_cols)
@@ -314,12 +321,12 @@
     blocks(trows // WIN + 1, groups1, 1)
 
     def feed1(i, _):
-        r = 7 * i
-        h = h2[pl.ds(4 + r, 7), 8 : 8 + tcols, :].reshape(7 * tcols, 128)
-        out_ref[pl.ds(r, 7)] = feed(1, h).astype(BF16).reshape(7, tcols, 128)
+        r = 14 * i
+        h = h2[pl.ds(4 + r, 14), 8 : 8 + tcols, :].reshape(14 * tcols, 128)
+        out_ref[pl.ds(r, 14)] = feed(1, h).astype(BF16).reshape(14, tcols, 128)
         return 0
 
-    lax.fori_loop(0, trows // 7, feed1, 0)
+    lax.fori_loop(0, trows // 14, feed1, 0)
 
 
 def prepare(
@@ -372,7 +379,7 @@
                 spread = ((row == 8 * (a + p) + plane) & (channel < 4)).astype(BF16)
                 total = total + dot(spread, taps[3 * a + b])
             blocks.append(total)
-    row = lax.broadcasted_iota(jnp.int32, (32, 128), 0)
+    row = lax.broadcasted_iota(jnp.int32, (32, C), 0)
     for p in range(2):
         blocks.append((row == 8 * (1 + p) + 4).astype(F32))
     wst_ref[...] = jnp.concatenate(blocks, 1).astype(BF16)
@@ -422,7 +429,7 @@
     return pl.pallas_call(
         prepare,
         out_shape=[
-            jax.ShapeDtypeStruct((32, 6 * C + 2 * D), BF16),
+            jax.ShapeDtypeStruct((32, 8 * C), BF16),
             jax.ShapeDtypeStruct((LAYERS - 1, 4 * C, 6 * C), BF16),
             jax.ShapeDtypeStruct((4 * C, 2 * D), BF16),
             jax.ShapeDtypeStruct((2, 56, HEADS * 64), F32),
@@ -437,7 +444,7 @@
                 pl.BlockSpec((2, 4, 169), lambda i, p, c: (0, 0, 0)),
             ],
             out_specs=[
-                pl.BlockSpec((32, 6 * C + 2 * D), lambda i, p, c: (0, 0)),
+                pl.BlockSpec((32, 8 * C), lambda i, p, c: (0, 0)),
                 pl.BlockSpec((LAYERS - 1, 4 * C, 6 * C), lambda i, p, c: (0, 0, 0)),
                 pl.BlockSpec((4 * C, 2 * D), lambda i, p, c: (0, 0)),
                 pl.BlockSpec((2, 56, HEADS * 64), lambda i, p, c: (0, 0, 0)),
@@ -531,19 +538,19 @@
     own = jnp.concatenate([planes.swapaxes(0, 1), labels.astype(BF16)[:, None]], 1)
     pair = swaps(own, "row")
     ready = prepared(pattern, candidate, stem_bank, layer_bank, embed_weight, rel_table)
-    pair, (wst, wl, e2, bias) = lax.optimization_barrier((pair, ready))
+    pair, (wst, wl, e2, bias) = (pair, ready)
     above, below = ordered(pair, "row")
     tall = jnp.concatenate([above[trows - RIM :], own, below[:RIM]], 0)
     ends = jnp.concatenate([tall[:, :, :RIM], tall[:, :, tcols - RIM :]], 2)
-    left, right = ordered(swaps(ends, "col"), "col")
+    first, second = swaps(ends, "col")
     place = jnp.stack([lax.axis_index("row"), lax.axis_index("col")]).astype(jnp.int32)
 
     return computed(
         (trows, tcols, nrows, ncols),
         place,
         tall,
-        left,
-        right,
+        first,
+        second,
         wst,
         e2,
         norm_gains,

time: 69.1 us -> 59.3 us (0.86)
  the two profiles are of different devices: /device:TPU:1 before, /device:TPU:8 now
where the time goes in v2:
time: 59.3 us; the launch traced here: 58.9 us
  Pallas kernels  41.4 us (70%)
  starting transfers between devices  12.7 us (21%)
  other arithmetic  2.9 us (5%)
  between operations  0.88 us (1%)
  local copies, waits for them, and re-layouts  0.73 us (1%)
    pallas_call x1, Pallas kernels, computed(): pl.pallas_call(functools.partial(kernel, *sizes), out_shape=jax.ShapeDtyp...  38 us
    ppermute x4, starting transfers between devices, swaps(): return (lax.ppermute(values, axis, even), lax.ppermute(values, axis, odd))  12.7 us
    pallas_call x1, Pallas kernels, prepared(): pl.pallas_call(prepare, out_shape=[jax.ShapeDtypeStruct((32, 8 * C), BF16...  3.44 us
  transfers between devices with their start and end apart: 4, of which 1 were waited for; matrix products, arithmetic and copies ran while one was open for 1% of the time, Pallas kernels for 6%

profile of v2, /device:TPU:8, one launch (start us, length us, event | category | flops | bytes accessed | tf_op | source)
XLA Modules:
  0.0 58.9 jit_solution(2073045211020680933)
XLA Ops:
  0.0 0.7 %convert_bitcast_fusion = bf16[14,1,112]{2,0,1:T(8,128)(2,1)S(1)} fusion(s32[14,112]{1,0:T(8,128)} %param.25), kind=kLoop, calls=%fused_computation.5 | loop fusion | flops 1568 | bytes 9408 | tf_op jit(solution)/shard_map/broadcast_in_dim | solution.py:538
  0.7 0.7 %pad_maximum_fusion.2 = bf16[14,5,112]{2,1,0:T(8,128)(2,1)S(1)} fusion(bf16[14,1,112]{2,1,0:T(2,128)(2,1)S(1)} %copy.20, bf16[14,4,112]{2,1,0:T(4,128)(2,1)} %bitcast.6), kind=kLoop, calls=%fused_computation.2 | loop fusion | flops 31360 | bytes 31360 | tf_op jit(solution)/shard_map/concatenate | solution.py:538
  1.5 0.1 collective-permute-start.1
  1.6 8.6 %collective-permute-start = (bf16[14,5,112]{2,1,0:T(8,128)(2,1)S(1)}, bf16[14,5,112]{2,1,0:T(8,128)(2,1)S(1)}, u32[]{:S(2)}, u32[]{:S(2)}) collective-permute-start(bf16[14,5,112]{2,1,0:T(8,128)(2,1)S(1)} %pad_maximum_fusion.2), channel_id=1, source_target_pairs={{0,248},{8,16},{16,8},{24,32},{32,24},{40,48},{48,40},{56,64},{64,... | collective-permute-start | bytes 47048 | tf_op jit(solution)/shard_map/ppermute | solution.py:476
  10.1 0.6 %pad_add_fusion.place_ref = s32[2]{0:T(128)} fusion(s32[1]{0:T(128)} %bitcast.1, s32[1]{0:T(128)} %bitcast), kind=kLoop, calls=%fused_computation.6 | loop fusion | flops 2 | bytes 16 | tf_op jit(solution)/shard_map/stack | solution.py:546
  11.4 0.0 collective-permute-done.1
  11.4 0.3 collective-permute-done
  11.7 0.7 %pad_maximum_fusion.tall_ref = bf16[38,5,112]{2,1,0:T(8,128)(2,1)S(1)} fusion(bf16[12,5,112]{2,1,0:T(8,128)(2,1)S(1)} %get-tuple-element.16, bf16[14,1,112]{2,1,0:T(2,128)(2,1)S(1)} %copy.20, bf16[14,4,112]{2,1,0:T(4,128)(2,1)} %bitcast.7, bf16[12,5,112]{2,1,0:T(8,128)(2,1)S(1)} %get-tuple-element.15), kind=kLoop, calls=%fused_computation | loop fusion | flops 170240 | bytes 85120 | tf_op jit(solution)/shard_map/concatenate | solution.py:543
  12.5 0.0 copy-start
  12.5 0.1 fusion
  12.6 0.1 pad_maximum_fusion.1
  12.7 1.7 %collective-permute-start.3 = (bf16[38,5,24]{2,1,0:T(8,128)(2,1)S(1)}, bf16[38,5,24]{2,1,0:T(8,128)(2,1)S(1)}, u32[]{:S(2)}, u32[]{:S(2)}) collective-permute-start(bf16[38,5,24]{2,1,0:T(8,128)(2,1)S(1)} %pad_maximum_fusion.1), channel_id=1, source_target_pairs={{0,7},{1,2},{2,1},{3,4},{4,3},{5,6},{6,5},{7,0},{8,15},{9,10},{10,... | collective-permute-start | bytes 27368 | tf_op jit(solution)/shard_map/ppermute | solution.py:476
  14.3 2.3 %collective-permute-start.2 = (bf16[38,5,24]{2,1,0:T(8,128)(2,1)S(1)}, bf16[38,5,24]{2,1,0:T(8,128)(2,1)S(1)}, u32[]{:S(2)}, u32[]{:S(2)}) collective-permute-start(bf16[38,5,24]{2,1,0:T(8,128)(2,1)S(1)} %pad_maximum_fusion.1), channel_id=1, source_target_pairs={{0,1},{1,0},{2,3},{3,2},{4,5},{5,4},{6,7},{7,6},{8,9},{9,8},{10,11... | collective-permute-start | bytes 27368 | tf_op jit(solution)/shard_map/ppermute | solution.py:476
  16.7 3.4 %shard_map.127 = (bf16[32,512]{1,0:T(8,128)(2,1)}, bf16[4,256,384]{2,1,0:T(8,128)(2,1)}, bf16[256,256]{1,0:T(8,128)(2,1)}, f32[2,56,256]{2,1,0:T(8,128)}) custom-call(s32[1]{0:T(128)S(6)} %copy.21.pattern_ref, s32[5]{0:T(128)} %_.1, bf16[4,9,4,64]{3,2,1,0:T(4,128)(2,1)} %bitcast.8, bf16[4,4,9,64,64]{4,3,2,1,0:T(8,128)(2,1)} %layer3_ref.1, ...), custom_call_target="tpu_custom_call" | custom-call | flops 100000000 | bytes 4000000 | tf_op jit(solution)/shard_map/pallas_call | solution.py:429
  20.1 0.0 copy-done
  20.1 0.0 collective-permute-done.3.second_ref
  20.1 0.0 copy-start.1
  20.1 0.0 collective-permute-done.2.first_ref
  20.1 0.0 copy-start.2
  20.2 0.6 %copy-done.1 = bf16[38,5,24]{2,1,0:T(8,128)(2,1)} copy-done((bf16[38,5,24]{2,1,0:T(8,128)(2,1)}, bf16[38,5,24]{2,1,0:T(8,128)(2,1)S(1)}, u32[]{:S(2)}) %copy-start.1) | copy-done | bytes 9144
  20.8 0.0 copy-done.2
  20.8 38.0 %shard_map.128 = bf16[14,112,128]{2,1,0:T(8,128)(2,1)} custom-call(s32[2]{0:T(128)} %pad_add_fusion.place_ref, bf16[38,5,112]{2,1,0:T(8,128)(2,1)} %copy-done, bf16[38,5,24]{2,1,0:T(8,128)(2,1)} %copy-done.2, bf16[38,5,24]{2,1,0:T(8,128)(2,1)} %copy-done.1, bf16[32,512]{1,0:T(8,128)(2,1)} %get-tuple-element.9.wst_ref, ...), custom_call_target="tpu_custom_call" | custom-call | tf_op jit(solution)/shard_map/pallas_call | solution.py:491
  (2 shorter events, 0.0 us)
Async XLA Ops:
  1.5 10.0 %collective-permute-start.1 = (bf16[14,5,112]{2,1,0:T(8,128)(2,1)S(1)}, bf16[14,5,112]{2,1,0:T(8,128)(2,1)S(1)}, u32[]{:S(2)}, u32[]{:S(2)}) collective-permute-start(bf16[14,5,112]{2,1,0:T(8,128)(2,1)S(1)} %pad_maximum_fusion.2), channel_id=1, source_target_pairs={{0,8},{8,0},{16,24},{24,16},{32,40},{40,32},{48,56},{56,48},{64,72... | collective-permute-start | bytes 47048 | tf_op jit(solution)/shard_map/ppermute | solution.py:476
  1.6 10.2 %collective-permute-start = (bf16[14,5,112]{2,1,0:T(8,128)(2,1)S(1)}, bf16[14,5,112]{2,1,0:T(8,128)(2,1)S(1)}, u32[]{:S(2)}, u32[]{:S(2)}) collective-permute-start(bf16[14,5,112]{2,1,0:T(8,128)(2,1)S(1)} %pad_maximum_fusion.2), channel_id=1, source_target_pairs={{0,248},{8,16},{16,8},{24,32},{32,24},{40,48},{48,40},{56,64},{64,... | collective-permute-start | bytes 47048 | tf_op jit(solution)/shard_map/ppermute | solution.py:476
  12.5 7.7 %copy-start = (bf16[38,5,112]{2,1,0:T(8,128)(2,1)}, bf16[38,5,112]{2,1,0:T(8,128)(2,1)S(1)}, u32[]{:S(2)}) copy-start(bf16[38,5,112]{2,1,0:T(8,128)(2,1)S(1)} %pad_maximum_fusion.tall_ref) | copy-start | bytes 127684
  12.7 7.4 %collective-permute-start.3 = (bf16[38,5,24]{2,1,0:T(8,128)(2,1)S(1)}, bf16[38,5,24]{2,1,0:T(8,128)(2,1)S(1)}, u32[]{:S(2)}, u32[]{:S(2)}) collective-permute-start(bf16[38,5,24]{2,1,0:T(8,128)(2,1)S(1)} %pad_maximum_fusion.1), channel_id=1, source_target_pairs={{0,7},{1,2},{2,1},{3,4},{4,3},{5,6},{6,5},{7,0},{8,15},{9,10},{10,... | collective-permute-start | bytes 27368 | tf_op jit(solution)/shard_map/ppermute | solution.py:476
  14.3 5.8 %collective-permute-start.2 = (bf16[38,5,24]{2,1,0:T(8,128)(2,1)S(1)}, bf16[38,5,24]{2,1,0:T(8,128)(2,1)S(1)}, u32[]{:S(2)}, u32[]{:S(2)}) collective-permute-start(bf16[38,5,24]{2,1,0:T(8,128)(2,1)S(1)} %pad_maximum_fusion.1), channel_id=1, source_target_pairs={{0,1},{1,0},{2,3},{3,2},{4,5},{5,4},{6,7},{7,6},{8,9},{9,8},{10,11... | collective-permute-start | bytes 27368 | tf_op jit(solution)/shard_map/ppermute | solution.py:476
  20.1 0.6 %copy-start.1 = (bf16[38,5,24]{2,1,0:T(8,128)(2,1)}, bf16[38,5,24]{2,1,0:T(8,128)(2,1)S(1)}, u32[]{:S(2)}) copy-start(bf16[38,5,24]{2,1,0:T(8,128)(2,1)S(1)} %collective-permute-done.3.second_ref) | copy-start | bytes 27364
  20.1 0.6 %copy-start.2 = (bf16[38,5,24]{2,1,0:T(8,128)(2,1)}, bf16[38,5,24]{2,1,0:T(8,128)(2,1)S(1)}, u32[]{:S(2)}) copy-start(bf16[38,5,24]{2,1,0:T(8,128)(2,1)S(1)} %collective-permute-done.2.first_ref) | copy-start | bytes 27364

commit v3 on v2

--- a/solution.py
+++ b/solution.py
@@ -514,7 +514,7 @@
             pltpu.VMEM((trows + WIN, fcols, 128), F32),
             pltpu.VMEM((8, 128), F32),
         ],
-        compiler_params=pltpu.CompilerParams(vmem_limit_bytes=VMEM),
+        compiler_params=pltpu.CompilerParams(vmem_limit_bytes=40 * 1024 * 1024),
     )(*arrays)
 
 
@@ -538,7 +538,7 @@
     own = jnp.concatenate([planes.swapaxes(0, 1), labels.astype(BF16)[:, None]], 1)
     pair = swaps(own, "row")
     ready = prepared(pattern, candidate, stem_bank, layer_bank, embed_weight, rel_table)
-    pair, (wst, wl, e2, bias) = (pair, ready)
+    wst, wl, e2, bias = ready
     above, below = ordered(pair, "row")
     tall = jnp.concatenate([above[trows - RIM :], own, below[:RIM]], 0)
     ends = jnp.concatenate([tall[:, :, :RIM], tall[:, :, tcols - RIM :]], 2)

time: 59.3 us -> 62.6 us (1.056)
  local copies, waits for them, and re-layouts: 0.73 us -> 3.81 us
    unnamed x6 -> x18, local copies, waits for them, and re-layouts: 0.63 us -> 3.71 us
  transfers between devices with their start and end apart: 4 -> 4, of which waited for: 1 -> 1; matrix products, arithmetic and copies ran while one was open for 1% -> 0% of each run, Pallas kernels for 6% -> 6%
where the time goes in v3:
time: 62.6 us; the launch traced here: 62.2 us
  Pallas kernels  41.6 us (66%)
  starting transfers between devices  12.7 us (20%)
  local copies, waits for them, and re-layouts  3.81 us (6%)
  other arithmetic  2.37 us (4%)
  between operations  0.91 us (1%)
  waiting for transfers between devices  0.83 us (1%)
    pallas_call x1, Pallas kernels, computed(): pl.pallas_call(functools.partial(kernel, *sizes), out_shape=jax.ShapeDtyp...  38 us
    ppermute x4, starting transfers between devices, swaps(): return (lax.ppermute(values, axis, even), lax.ppermute(values, axis, odd))  12.7 us
    unnamed x18, local copies, waits for them, and re-layouts  3.71 us
    pallas_call x1, Pallas kernels, prepared(): pl.pallas_call(prepare, out_shape=[jax.ShapeDtypeStruct((32, 8 * C), BF16...  3.56 us
  transfers between devices with their start and end apart: 4, of which 1 were waited for; matrix products, arithmetic and copies ran while one was open for 0% of the time, Pallas kernels for 6%

profile of v3, /device:TPU:8, one launch (start us, length us, event | category | flops | bytes accessed | tf_op | source)
XLA Modules:
  0.0 62.2 jit_solution(12575457596468448412)
XLA Ops:
  0.0 0.7 %convert_bitcast_fusion = bf16[14,1,112]{2,0,1:T(8,128)(2,1)S(1)} fusion(s32[14,112]{1,0:T(8,128)} %param.25), kind=kLoop, calls=%fused_computation.5 | loop fusion | flops 1568 | bytes 9408 | tf_op jit(solution)/shard_map/broadcast_in_dim | solution.py:538
  0.7 0.7 %pad_maximum_fusion.2 = bf16[14,5,112]{2,1,0:T(8,128)(2,1)S(1)} fusion(bf16[14,1,112]{2,1,0:T(2,128)(2,1)S(1)} %copy.20, bf16[14,4,112]{2,1,0:T(4,128)(2,1)} %bitcast.6), kind=kLoop, calls=%fused_computation.2 | loop fusion | flops 31360 | bytes 31360 | tf_op jit(solution)/shard_map/concatenate | solution.py:538
  1.5 0.1 collective-permute-start.1
  1.6 8.6 %collective-permute-start = (bf16[14,5,112]{2,1,0:T(8,128)(2,1)S(1)}, bf16[14,5,112]{2,1,0:T(8,128)(2,1)S(1)}, u32[]{:S(2)}, u32[]{:S(2)}) collective-permute-start(bf16[14,5,112]{2,1,0:T(8,128)(2,1)S(1)} %pad_maximum_fusion.2), channel_id=1, source_target_pairs={{0,248},{8,16},{16,8},{24,32},{32,24},{40,48},{48,40},{56,64},{64,... | collective-permute-start | bytes 47048 | tf_op jit(solution)/shard_map/ppermute | solution.py:476
  10.1 0.1 pad_add_fusion.place_ref
  10.9 0.0 collective-permute-done.1
  10.9 0.8 %collective-permute-done = bf16[14,5,112]{2,1,0:T(8,128)(2,1)S(1)} collective-permute-done((bf16[14,5,112]{2,1,0:T(8,128)(2,1)S(1)}, bf16[14,5,112]{2,1,0:T(8,128)(2,1)S(1)}, u32[]{:S(2)}, u32[]{:S(2)}) %collective-permute-start) | collective-permute-done | bytes 15712 | tf_op jit(solution)/shard_map/ppermute | solution.py:476
  11.7 0.7 %pad_maximum_fusion.tall_ref = bf16[38,5,112]{2,1,0:T(8,128)(2,1)S(1)} fusion(bf16[12,5,112]{2,1,0:T(8,128)(2,1)S(1)} %get-tuple-element.16, bf16[14,1,112]{2,1,0:T(2,128)(2,1)S(1)} %copy.20, bf16[14,4,112]{2,1,0:T(4,128)(2,1)} %bitcast.7, bf16[12,5,112]{2,1,0:T(8,128)(2,1)S(1)} %get-tuple-element.15), kind=kLoop, calls=%fused_computation | loop fusion | flops 170240 | bytes 85120 | tf_op jit(solution)/shard_map/concatenate | solution.py:543
  12.5 0.1 fusion
  12.6 0.1 pad_maximum_fusion.1
  12.7 1.7 %collective-permute-start.3 = (bf16[38,5,24]{2,1,0:T(8,128)(2,1)S(1)}, bf16[38,5,24]{2,1,0:T(8,128)(2,1)S(1)}, u32[]{:S(2)}, u32[]{:S(2)}) collective-permute-start(bf16[38,5,24]{2,1,0:T(8,128)(2,1)S(1)} %pad_maximum_fusion.1), channel_id=1, source_target_pairs={{0,7},{1,2},{2,1},{3,4},{4,3},{5,6},{6,5},{7,0},{8,15},{9,10},{10,... | collective-permute-start | bytes 27368 | tf_op jit(solution)/shard_map/ppermute | solution.py:476
  14.3 2.3 %collective-permute-start.2 = (bf16[38,5,24]{2,1,0:T(8,128)(2,1)S(1)}, bf16[38,5,24]{2,1,0:T(8,128)(2,1)S(1)}, u32[]{:S(2)}, u32[]{:S(2)}) collective-permute-start(bf16[38,5,24]{2,1,0:T(8,128)(2,1)S(1)} %pad_maximum_fusion.1), channel_id=1, source_target_pairs={{0,1},{1,0},{2,3},{3,2},{4,5},{5,4},{6,7},{7,6},{8,9},{9,8},{10,11... | collective-permute-start | bytes 27368 | tf_op jit(solution)/shard_map/ppermute | solution.py:476
  16.7 0.0 copy-start.8
  16.7 3.6 %shard_map.127 = (bf16[32,512]{1,0:T(8,128)(2,1)}, bf16[4,256,384]{2,1,0:T(8,128)(2,1)}, bf16[256,256]{1,0:T(8,128)(2,1)}, f32[2,56,256]{2,1,0:T(8,128)}) custom-call(s32[1]{0:T(128)S(6)} %copy.21.pattern_ref, s32[5]{0:T(128)} %_.1, bf16[4,9,4,64]{3,2,1,0:T(4,128)(2,1)} %bitcast.8, bf16[4,4,9,64,64]{4,3,2,1,0:T(8,128)(2,1)} %layer3_ref.1, ...), custom_call_target="tpu_custom_call" | custom-call | flops 100000000 | bytes 4000000 | tf_op jit(solution)/shard_map/pallas_call | solution.py:429
  20.3 0.0 collective-permute-done.3.second_ref
  20.3 0.0 collective-permute-done.2.first_ref
  20.3 0.0 copy-done.1
  20.3 0.0 copy-done.2
  20.3 0.0 copy-done.3
  20.3 1.1 %copy-done = bf16[4,256,384]{2,1,0:T(8,128)(2,1)S(1)} copy-done((bf16[4,256,384]{2,1,0:T(8,128)(2,1)S(1)}, bf16[4,256,384]{2,1,0:T(8,128)(2,1)}, u32[]{:S(2)}) %copy-start) | copy-done | bytes 786456
  21.5 0.9 %copy-done.4 = bf16[256,256]{1,0:T(8,128)(2,1)S(1)} copy-done((bf16[256,256]{1,0:T(8,128)(2,1)S(1)}, bf16[256,256]{1,0:T(8,128)(2,1)}, u32[]{:S(2)}) %copy-start.4) | copy-done | bytes 131096
  22.4 0.9 %copy-done.5 = f32[2,56,256]{2,1,0:T(8,128)S(1)} copy-done((f32[2,56,256]{2,1,0:T(8,128)S(1)}, f32[2,56,256]{2,1,0:T(8,128)}, u32[]{:S(2)}) %copy-start.5) | copy-done | bytes 114712
  23.3 0.8 %copy-done.7 = bf16[32,512]{1,0:T(8,128)(2,1)S(1)} copy-done((bf16[32,512]{1,0:T(8,128)(2,1)S(1)}, bf16[32,512]{1,0:T(8,128)(2,1)}, u32[]{:S(2)}) %copy-start.7) | copy-done | bytes 32792
  24.0 38.0 %shard_map.128 = bf16[14,112,128]{2,1,0:T(8,128)(2,1)} custom-call(s32[2]{0:T(128)S(1)} %pad_add_fusion.place_ref, bf16[38,5,112]{2,1,0:T(8,128)(2,1)S(1)} %pad_maximum_fusion.tall_ref, bf16[38,5,24]{2,1,0:T(8,128)(2,1)S(1)} %collective-permute-done.2.first_ref, bf16[38,5,24]{2,1,0:T(8,128)(2,1)S(1)} %collective-permute-done.3.second_ref, ...), custom_call_target="tpu_custom_call" | custom-call | tf_op jit(solution)/shard_map/pallas_call | solution.py:491
  (12 shorter events, 0.0 us)
Async XLA Ops:
  1.5 9.4 %collective-permute-start.1 = (bf16[14,5,112]{2,1,0:T(8,128)(2,1)S(1)}, bf16[14,5,112]{2,1,0:T(8,128)(2,1)S(1)}, u32[]{:S(2)}, u32[]{:S(2)}) collective-permute-start(bf16[14,5,112]{2,1,0:T(8,128)(2,1)S(1)} %pad_maximum_fusion.2), channel_id=1, source_target_pairs={{0,8},{8,0},{16,24},{24,16},{32,40},{40,32},{48,56},{56,48},{64,72... | collective-permute-start | bytes 47048 | tf_op jit(solution)/shard_map/ppermute | solution.py:476
  1.6 10.2 %collective-permute-start = (bf16[14,5,112]{2,1,0:T(8,128)(2,1)S(1)}, bf16[14,5,112]{2,1,0:T(8,128)(2,1)S(1)}, u32[]{:S(2)}, u32[]{:S(2)}) collective-permute-start(bf16[14,5,112]{2,1,0:T(8,128)(2,1)S(1)} %pad_maximum_fusion.2), channel_id=1, source_target_pairs={{0,248},{8,16},{16,8},{24,32},{32,24},{40,48},{48,40},{56,64},{64,... | collective-permute-start | bytes 47048 | tf_op jit(solution)/shard_map/ppermute | solution.py:476
  12.7 7.6 %collective-permute-start.3 = (bf16[38,5,24]{2,1,0:T(8,128)(2,1)S(1)}, bf16[38,5,24]{2,1,0:T(8,128)(2,1)S(1)}, u32[]{:S(2)}, u32[]{:S(2)}) collective-permute-start(bf16[38,5,24]{2,1,0:T(8,128)(2,1)S(1)} %pad_maximum_fusion.1), channel_id=1, source_target_pairs={{0,7},{1,2},{2,1},{3,4},{4,3},{5,6},{6,5},{7,0},{8,15},{9,10},{10,... | collective-permute-start | bytes 27368 | tf_op jit(solution)/shard_map/ppermute | solution.py:476
  14.3 5.9 %collective-permute-start.2 = (bf16[38,5,24]{2,1,0:T(8,128)(2,1)S(1)}, bf16[38,5,24]{2,1,0:T(8,128)(2,1)S(1)}, u32[]{:S(2)}, u32[]{:S(2)}) collective-permute-start(bf16[38,5,24]{2,1,0:T(8,128)(2,1)S(1)} %pad_maximum_fusion.1), channel_id=1, source_target_pairs={{0,1},{1,0},{2,3},{3,2},{4,5},{5,4},{6,7},{7,6},{8,9},{9,8},{10,11... | collective-permute-start | bytes 27368 | tf_op jit(solution)/shard_map/ppermute | solution.py:476
  16.7 3.6 %copy-start.1 = (bf16[2,128,512]{2,1,0:T(8,128)(2,1)S(1)}, bf16[2,128,512]{2,1,0:T(8,128)(2,1)}, u32[]{:S(2)}) copy-start(bf16[2,128,512]{2,1,0:T(8,128)(2,1)} %fc1_hbm.1) | copy-start | bytes 786436
  16.7 3.6 %copy-start.2 = (bf16[2,512,128]{2,1,0:T(8,128)(2,1)S(1)}, bf16[2,512,128]{2,1,0:T(8,128)(2,1)}, u32[]{:S(2)}) copy-start(bf16[2,512,128]{2,1,0:T(8,128)(2,1)} %fc2_hbm.1) | copy-start | bytes 786436
  16.7 3.6 %copy-start.3 = (bf16[2,128,384]{2,1,0:T(8,128)(2,1)S(1)}, bf16[2,128,384]{2,1,0:T(8,128)(2,1)}, u32[]{:S(2)}) copy-start(bf16[2,128,384]{2,1,0:T(8,128)(2,1)} %qkv_hbm.1) | copy-start | bytes 589828
  16.7 3.6 %copy-start.6 = (bf16[2,128,128]{2,1,0:T(8,128)(2,1)S(1)}, bf16[2,128,128]{2,1,0:T(8,128)(2,1)}, u32[]{:S(2)}) copy-start(bf16[2,128,128]{2,1,0:T(8,128)(2,1)} %proj_hbm.1) | copy-start | bytes 196612
  16.7 3.6 %copy-start.8 = (f32[5,128]{1,0:T(8,128)S(1)}, f32[5,128]{1,0:T(8,128)}, u32[]{:S(2)}) copy-start(f32[5,128]{1,0:T(8,128)} %gains_ref.1) | copy-start | bytes 7684
  20.3 1.1 %copy-start = (bf16[4,256,384]{2,1,0:T(8,128)(2,1)S(1)}, bf16[4,256,384]{2,1,0:T(8,128)(2,1)}, u32[]{:S(2)}) copy-start(bf16[4,256,384]{2,1,0:T(8,128)(2,1)} %get-tuple-element.11.wl_hbm) | copy-start | bytes 2359300
  21.4 0.9 %copy-start.4 = (bf16[256,256]{1,0:T(8,128)(2,1)S(1)}, bf16[256,256]{1,0:T(8,128)(2,1)}, u32[]{:S(2)}) copy-start(bf16[256,256]{1,0:T(8,128)(2,1)} %get-tuple-element.10.e2_ref) | copy-start | bytes 393220
  22.4 0.9 %copy-start.5 = (f32[2,56,256]{2,1,0:T(8,128)S(1)}, f32[2,56,256]{2,1,0:T(8,128)}, u32[]{:S(2)}) copy-start(f32[2,56,256]{2,1,0:T(8,128)} %get-tuple-element.12.bias_hbm) | copy-start | bytes 344068
  23.3 0.8 %copy-start.7 = (bf16[32,512]{1,0:T(8,128)(2,1)S(1)}, bf16[32,512]{1,0:T(8,128)(2,1)}, u32[]{:S(2)}) copy-start(bf16[32,512]{1,0:T(8,128)(2,1)} %get-tuple-element.9.wst_ref) | copy-start | bytes 98308
